TPU v7x, 32 devices: a whole 2x2x4 slice. The times are simulated.
32 devices in a mesh: batch: 4 (over y, core), rows: 8 (over z, x).
Axes of the slice: x: 2, y: 2, z: 4, core: 2. Of those that a mesh axis runs over, the one named last changes fastest.
Arguments:
- features_0: bfloat16 [4, 48, 128, 256], P('batch', None, 'rows'), may hold values from -6 to 6
- features_1: bfloat16 [4, 96, 64, 128], P('batch', None, 'rows'), may hold values from -6 to 6
- features_2: bfloat16 [4, 192, 32, 64], P('batch', None, 'rows'), may hold values from -6 to 6
- features_3: bfloat16 [4, 384, 16, 32], P('batch', None, 'rows'), may hold values from -6 to 6
- block_0: bfloat16 [2, 3, 3, 48, 48], replicated, may hold values from -0.3125 to 0.3125
- block_1: bfloat16 [2, 3, 3, 96, 96], replicated, may hold values from -0.21875 to 0.21875
- block_2: bfloat16 [2, 3, 3, 192, 192], replicated, may hold values from -0.15625 to 0.15625
- block_3: bfloat16 [2, 3, 3, 384, 384], replicated, may hold values from -0.109375 to 0.109375
- unite_1: bfloat16 [48, 96], replicated, may hold values from -0.625 to 0.625
- unite_2: bfloat16 [48, 192], replicated, may hold values from -0.4375 to 0.4375
- unite_3: bfloat16 [48, 384], replicated, may hold values from -0.3125 to 0.3125
- norm_gains: float32 [2, 720], replicated, may hold values from 0.5 to 1.5
- norm_shifts: float32 [2, 720], replicated, may hold values from -3 to 3
- unite_gains: float32 [3, 48], replicated, may hold values from 0.5 to 1.5
- unite_shifts: float32 [3, 48], replicated, may hold values from -3 to 3
- output_grad: bfloat16 [4, 48, 128, 256], P('batch', None, 'rows'), may hold values from -6 to 6
- heights: int32 [4], replicated, may hold values from 8 to 128, as said below
- widths: int32 [4], replicated, may hold values from 8 to 256, as said below
- item_slot: int32 [4], replicated, may hold values from 0 to 3, each once
Outputs:
- united: bfloat16 [4, 48, 128, 256], P('batch', None, 'rows')
- grad_features_0: bfloat16 [4, 48, 128, 256], P('batch', None, 'rows')
- grad_features_1: bfloat16 [4, 96, 64, 128], P('batch', None, 'rows')
- grad_features_2: bfloat16 [4, 192, 32, 64], P('batch', None, 'rows')
- grad_features_3: bfloat16 [4, 384, 16, 32], P('batch', None, 'rows')
- grad_block_0: float32 [2, 3, 3, 48, 48], P(None, None, None, 'batch')
- grad_block_1: float32 [2, 3, 3, 96, 96], P(None, None, None, 'batch')
- grad_block_2: float32 [2, 3, 3, 192, 192], P(None, None, None, 'batch')
- grad_block_3: float32 [2, 3, 3, 384, 384], P(None, None, None, 'batch')
- grad_unite_1: float32 [48, 96], P('batch')
- grad_unite_2: float32 [48, 192], P('batch')
- grad_unite_3: float32 [48, 384], P('batch')
- grad_norm_gains: float32 [2, 720], replicated
- grad_norm_shifts: float32 [2, 720], replicated
- grad_unite_gains: float32 [3, 48], replicated
- grad_unite_shifts: float32 [3, 48], replicated
Inputs may be any that keep to these rules, and one draw needn't show every extreme that they name: `heights`: multiples of 8; in every draw some items are whole, with all 128 rows and all 256 columns. `widths`: multiples of 8. `item_slot`: a permutation of the slots.
All inputs are finite; a program needn't handle non-finite values.
Results may differ from a plain program's by a relative error of at most 0.018.
Values may be sent and summed in bfloat16 or wider, within the bound.
A program may use at most 128 MiB of HBM per device.

v0:
```python
import functools

import jax
import jax.numpy as jnp
import numpy as np
from jax import lax
from jax.experimental import pallas as pl
from jax.experimental.pallas import tpu as pltpu
from jax.sharding import PartitionSpec as P

EPSILON = 1e-05
LEVELS = 4
MESH = pl.DeviceIdType.MESH
F32 = jnp.float32
BF16 = jnp.bfloat16

MEAN, RSTD, GAIN1, SHIFT1, GAIN2, SHIFT2, LOCAL, N_COLS = range(8)
CA, CB, CC = MEAN, RSTD, LOCAL
UMEAN, URSTD, UGAIN, USHIFT, ULOCAL, UA, UB, UC, N_UCOLS = range(9)


class Sizes:
    def __init__(self, features, nb, nk):
        self.chan = [f.shape[1] for f in features]
        self.rows = [f.shape[2] for f in features]
        self.width = [f.shape[3] for f in features]
        self.own = [r * w for r, w in zip(self.rows, self.width)]
        self.flat = [(r + 2) * w for r, w in zip(self.rows, self.width)]
        self.off = [sum(self.chan[:l]) for l in range(LEVELS)]
        self.total = sum(self.chan)
        self.blocks = -(-self.total // 128)
        self.uchan = self.chan[0]
        self.utotal = 3 * self.uchan
        self.ublocks = -(-self.utotal // 128)
        self.rim_rows = [c * w // 128 for c, w in zip(self.chan, self.width)]
        self.rim_off = [sum(self.rim_rows[:l]) for l in range(LEVELS)]
        self.rim_total = sum(self.rim_rows)
        self.chunk = []
        for c, n, w in zip(self.chan, self.flat, self.width):
            lanes = max(x for x in range(128, 641, 128) if n % x == 0 and x % w == 0)
            rows = max(r for r in (16, 32, 48) if c % r == 0 and r * lanes <= 12288)
            self.chunk.append((rows, lanes))
        self.nc = 2 if nb % 2 == 0 else 1
        self.nx = 2 if nk % 2 == 0 else 1
        self.ny = nb // self.nc
        self.nz = nk // self.nx
        self.gather = nb * nk <= 32 and self.nx == 2 and self.nc == 2 and self.own[3] == 64
        self.sum_levels = [0, 1, 2]
        self.stacked = [l for l in range(3 if self.gather else 4) if self.width[l] < 128]
        self.spots = {}
        at = 0
        for l in self.sum_levels:
            rows = -(-3 * self.chan[l] // nb // 16) * 16
            for i in range(-(-3 * self.chan[l] // 128)):
                self.spots[l, i] = (at, rows)
                at += rows
        for j in range(3):
            rows = -(-self.uchan // nb // 16) * 16
            for i in range(-(-self.chan[j + 1] // 128)):
                self.spots["u", j, i] = (at, rows)
                at += rows
        self.part = -(-at // (nk * 16)) * 16
        self.sum_rows = self.part * nk


def blend(scale, rows):
    out = []
    for g in range(rows):
        num = 2 * g + 1 - scale
        low = num // (2 * scale)
        out.append((low + 1, (num - 2 * scale * low) / (2.0 * scale)))
    return out


def column_table(width, fine):
    scale = fine // width
    group = max(1, 128 // width)
    span = max(128, width)
    table = np.zeros((span, group * fine), np.float32)
    for r in range(group):
        for g in range(fine):
            num = 2 * g + 1 - scale
            low = 0 if num < 0 else num // (2 * scale)
            frac = 0.0 if num < 0 else (num - 2 * scale * low) / (2.0 * scale)
            high = min(low + 1, width - 1)
            table[r * width + low, r * fine + g] += 1.0 - frac
            table[r * width + high, r * fine + g] += frac
    return table


def sigmoid(v):
    return jax.nn.sigmoid(v)


def main_kernel(sz, nb, nk, *refs):
    it = iter(refs)
    take = lambda n: [next(it) for _ in range(n)]
    heights, widths, slots = take(3)
    feats = take(4)
    (ograd,) = take(1)
    blocks = take(4)
    unites = take(3)
    norm_gains, norm_shifts, unite_gains, unite_shifts = take(4)
    tables = take(3)
    tables_t = take(3)
    (united_ref,) = take(1)
    gfeat = take(4)
    (sums_ref,) = take(1)
    (coarse_ref,) = take(1)
    (totals_ref,) = take(1)
    raw = take(3 if sz.gather else 4)
    wide = take(4)
    (stage,) = take(1)
    x3 = take(4)
    a3 = take(4)
    g3 = take(4)
    t3 = dict(zip(sz.stacked, take(len(sz.stacked))))
    cstage, cstage_sem = take(2)
    (kg,) = take(1)
    gun = take(3)
    xf = take(4)
    y1 = take(4)
    y2 = take(4)
    p1 = take(4)
    br = take(3)
    uo = take(3)
    up = take(3)
    (cols, ucols, stat_a, stat_b, ustat_a, ustat_b, n_a, n_b, un_a, un_b) = take(10)
    masks = take(4)
    (rec_a, rec_b, rim_s, rim_r, mid_s, mid_r) = take(6)
    (sa_send, sa_recv, sb_send, sb_recv, rim_send, rim_recv) = take(6)
    raw_sem, wide_sem = take(2)
    prow, urow = take(2)
    part_a, got_a, got_b, got_c, got_d, out_sem = take(6)
    (ra_send, ra_recv, rb_send, rb_recv, rc_send, rc_recv, rd_send, rd_recv) = take(8)
    if sz.gather:
        xg, gs, gr, x3g, t3g = take(5)
        (xg_send, xg_recv, g1_send, g1_recv, g2_send, g2_recv) = take(6)

    C, R, W, N, NP, OFF = sz.chan, sz.rows, sz.width, sz.own, sz.flat, sz.off
    me_b = lax.axis_index("batch")
    me_k = lax.axis_index("rows")

    def peer_b(j):
        return lax.rem(me_b + j, nb)

    def peer_k(j):
        return lax.rem(me_k + j, nk)

    def raw_copy(l, which):
        if l == 3 and sz.gather:
            dst = x3g.at[0:3, :, 0 : C[3]]
        else:
            dst = raw[l]
        return pltpu.make_async_copy(blocks[l].at[which], dst, raw_sem.at[l, which])

    def wide_copies(which):
        c = C[3]
        return [
            pltpu.make_async_copy(
                blocks[3].at[which, t, u * c : (u + 1) * c, :],
                wide[3].at[which, t * c : (t + 1) * c, u * c : (u + 1) * c],
                wide_sem.at[which, 3 * t + u],
            )
            for t in range(3)
            for u in range(3)
        ]

    for l in range(3):
        raw_copy(l, 0).start()
    for which in range(2):
        for copy in wide_copies(which):
            copy.start()
    raw_copy(3, 0).start()

    def widen(which):
        for copy in wide_copies(which):
            copy.wait()
        for l in range(3):
            raw_copy(l, which).wait()
            c = C[l]
            for t in range(3):
                wide[l][which, t * c : (t + 1) * c, :] = jnp.concatenate(
                    [raw[l][t, u * c : (u + 1) * c, :] for u in range(3)], axis=1
                )

    def turn(which):
        raw_copy(3, which).wait()
        for l in range(LEVELS):
            for t in range(3):
                if l == 3 and sz.gather:
                    v = x3g[t, :, 0 : C[3]]
                else:
                    v = raw[l][t]
                wide[l][which, t * C[l] : (t + 1) * C[l], :] = v.T
        if which == 0:
            for l in range(LEVELS):
                raw_copy(l, 1).start()

    barrier = pltpu.get_barrier_semaphore()
    for j in range(1, nb):
        pl.semaphore_signal(barrier, inc=1, device_id=(peer_b(j), me_k), device_id_type=MESH)
    for j in range(1, nk):
        pl.semaphore_signal(barrier, inc=1, device_id=(me_b, peer_k(j)), device_id_type=MESH)
    pl.semaphore_wait(barrier, nb + nk - 2)

    my_h = jnp.int32(0)
    my_w = jnp.int32(0)
    slot_h, slot_w = [], []
    for b in range(nb):
        h = jnp.int32(0)
        w = jnp.int32(0)
        for i in range(nb):
            hit = (slots[i] == b).astype(jnp.int32)
            h = h + hit * heights[i]
            w = w + hit * widths[i]
        slot_h.append(h)
        slot_w.append(w)
        mine = (me_b == b).astype(jnp.int32)
        my_h = my_h + mine * h
        my_w = my_w + mine * w

    count = []
    for l in range(LEVELS):
        c = jnp.int32(0)
        for b in range(nb):
            c = c + lax.shift_right_logical(slot_h[b], l) * lax.shift_right_logical(slot_w[b], l)
        count.append(c.astype(F32))
    inv_local = []
    for l in range(LEVELS):
        inside = jnp.clip(lax.shift_right_logical(my_h, l) - me_k * R[l], 0, R[l])
        own = inside * lax.shift_right_logical(my_w, l)
        inv_local.append(1.0 / jnp.maximum(own, 1).astype(F32))
        lane = lax.broadcasted_iota(jnp.int32, (1, NP[l]), 1)
        log_w = W[l].bit_length() - 1
        row = me_k * R[l] + lax.shift_right_logical(lane, log_w) - 1
        col = lane & (W[l] - 1)
        valid = (row >= 0) & (row < lax.shift_right_logical(my_h, l))
        valid = valid & (col < lax.shift_right_logical(my_w, l))
        masks[l][0:1, :] = jnp.where(valid, 1.0, 0.0)
        masks[l][1:2, :] = jnp.where(valid & (lane >= W[l]) & (lane < W[l] + N[l]), 1.0, 0.0)

    place = lax.broadcasted_iota(jnp.int32, (8, 128), 0) * 128 + lax.broadcasted_iota(
        jnp.int32, (8, 128), 1
    )

    def by_level(values):
        out = jnp.full((8, 128), values[3])
        for l in (2, 1, 0):
            out = jnp.where(place < OFF[l + 1], jnp.full((8, 128), values[l]), out)
        return out

    def by_unite(values):
        out = jnp.full((8, 128), values[2])
        for j in (1, 0):
            out = jnp.where(place < (j + 1) * sz.uchan, jnp.full((8, 128), values[j]), out)
        return out

    inv_count = 1.0 / by_level(count)
    inv_ucount = 1.0 / by_unite(count[1:])
    for chooser, levels, na_ref, nb_ref in (
        (by_level, range(4), n_a, n_b),
        (by_unite, range(1, 4), un_a, un_b),
    ):
        span = chooser([jnp.int32(R[l]) for l in levels])
        hv = [chooser([lax.shift_right_logical(h, l) for l in levels]) for h in slot_h]
        wv = [chooser([lax.shift_right_logical(w, l) for l in levels]) for w in slot_w]
        for b in range(nb):
            na_ref[b] = (jnp.clip(hv[b] - me_k * span, 0, span) * wv[b]).astype(F32)
        for k in range(nk):
            n = jnp.zeros((8, 128), jnp.int32)
            for b in range(nb):
                n = n + jnp.clip(hv[b] - k * span, 0, span) * wv[b]
            nb_ref[k] = n.astype(F32)

    def tile(v, lanes):
        return v if lanes == 128 else jnp.concatenate([v] * (lanes // 128), axis=1)

    def col(slot, l, r0, rc, lanes):
        return tile(cols[slot, pl.ds(pl.multiple_of(OFF[l] + r0, 16), rc), :], lanes)

    def ucol(slot, j, lanes):
        return tile(ucols[slot, j * sz.uchan : (j + 1) * sz.uchan, :], lanes)

    def to_columns(packed, ref, slot_list, blocks):
        full = jnp.concatenate(packed + [jnp.zeros((128 - 8 * len(packed), 128), F32)], axis=0)
        turned = full.T
        for i, slot in enumerate(slot_list):
            for k in range(blocks):
                ref[slot, 128 * k : 128 * k + 128, :] = jnp.broadcast_to(
                    turned[:, 8 * i + k : 8 * i + k + 1], (128, 128)
                )

    prow[...] = jnp.zeros_like(prow)
    urow[...] = jnp.zeros_like(urow)
    for i in range(2):
        prow[2 * i : 2 * i + 1, 0 : sz.total] = norm_gains[i : i + 1, :]
        prow[2 * i + 1 : 2 * i + 2, 0 : sz.total] = norm_shifts[i : i + 1, :]
    for j in range(3):
        at = slice(j * sz.uchan, (j + 1) * sz.uchan)
        urow[0:1, at] = unite_gains[j : j + 1, :]
        urow[1:2, at] = unite_shifts[j : j + 1, :]
    standing = prow[...].T
    for i, slot in enumerate((GAIN1, SHIFT1, GAIN2, SHIFT2)):
        cols[slot] = jnp.broadcast_to(standing[:, i : i + 1], (sz.blocks * 128, 128))
    standing = urow[...].T
    for i, slot in enumerate((UGAIN, USHIFT)):
        ucols[slot] = jnp.broadcast_to(standing[:, i : i + 1], (sz.ublocks * 128, 128))

    def packed(ref, i, blocks):
        rows = [ref[i : i + 1, 128 * k : 128 * k + 128] for k in range(blocks)]
        return jnp.concatenate(rows + [jnp.zeros((8 - blocks, 128), F32)], axis=0)

    gain1_p, gain2_p = packed(prow, 0, sz.blocks), packed(prow, 2, sz.blocks)
    ugain_p = packed(urow, 0, sz.ublocks)
    stat_a[...] = jnp.zeros_like(stat_a)
    stat_b[...] = jnp.zeros_like(stat_b)
    ustat_a[...] = jnp.zeros_like(ustat_a)
    ustat_b[...] = jnp.zeros_like(ustat_b)

    def fold(v):
        out = v[:, 0:128]
        for i in range(1, v.shape[1] // 128):
            out = out + v[:, 128 * i : 128 * i + 128]
        return out

    lane128 = lax.broadcasted_iota(jnp.int32, (1, 128), 1)

    def record(a_ref, b_ref, blocks):
        out = jnp.zeros((128, 128), F32)
        for base, ref in ((0, a_ref), (8, b_ref)):
            for k in range(blocks):
                s = jnp.sum(ref[128 * k : 128 * k + 128, :], axis=1, keepdims=True)
                out = jnp.where(lane128 == base + k, s, out)
        return out.T[0:16]

    def spread(e, which, rec, meanwhile):
        copies = []
        if which == 0:
            ref, send, recv, n, me = rec_a, sa_send, sa_recv, nb, me_b
        else:
            ref, send, recv, n, me = rec_b, sb_send, sb_recv, nk, me_k
        ref[e, me] = rec
        for j in range(1, n):
            target = (peer_b(j), me_k) if which == 0 else (me_b, peer_k(j))
            copy = pltpu.make_async_remote_copy(
                src_ref=ref.at[e, me],
                dst_ref=ref.at[e, me],
                send_sem=send.at[e, j],
                recv_sem=recv.at[e, me],
                device_id=target,
                device_id_type=MESH,
            )
            copy.start()
            copies.append(copy)
        if meanwhile is not None:
            meanwhile()
        for j in range(1, n):
            other = peer_b(j) if which == 0 else peer_k(j)
            pltpu.make_async_remote_copy(
                src_ref=ref.at[e, me],
                dst_ref=ref.at[e, other],
                send_sem=send.at[e, j],
                recv_sem=recv.at[e, other],
                device_id=(me_b, me_k),
                device_id_type=MESH,
            ).wait_recv()
        for copy in copies:
            copy.wait_send()

    def gather_moments(e, rec, na_ref, nb_ref, meanwhile=(None, None)):
        for which, n, ref, n_ref in ((0, nb, rec_a, na_ref), (1, nk, rec_b, nb_ref)):
            spread(e, which, rec, meanwhile[which])
            total = jnp.zeros((8, 128), F32)
            size = jnp.zeros((8, 128), F32)
            for i in range(n):
                total = total + ref[e, i, 0:8]
                size = size + n_ref[i]
            mean = total / jnp.maximum(size, 1.0)
            spread_sum = jnp.zeros((8, 128), F32)
            for i in range(n):
                delta = ref[e, i, 0:8] / jnp.maximum(n_ref[i], 1.0) - mean
                spread_sum = spread_sum + (ref[e, i, 8:16] + n_ref[i] * delta * delta)
            rec = jnp.concatenate([total, spread_sum], axis=0)
        return rec

    def gather_sums(e, rec, meanwhile=(None, None)):
        for which, n, ref in ((0, nb, rec_a), (1, nk, rec_b)):
            spread(e, which, rec, meanwhile[which])
            rec = jnp.zeros((16, 128), F32)
            for i in range(n):
                rec = rec + ref[e, i]
        return rec

    def rim_copies(slot, src, dst):
        up = pltpu.make_async_remote_copy(
            src_ref=src.at[0],
            dst_ref=dst.at[1],
            send_sem=rim_send.at[slot, 0],
            recv_sem=rim_recv.at[slot, 1],
            device_id=(me_b, lax.rem(me_k + nk - 1, nk)),
            device_id_type=MESH,
        )
        down = pltpu.make_async_remote_copy(
            src_ref=src.at[1],
            dst_ref=dst.at[0],
            send_sem=rim_send.at[slot, 1],
            recv_sem=rim_recv.at[slot, 0],
            device_id=(me_b, lax.rem(me_k + 1, nk)),
            device_id_type=MESH,
        )
        return up, down

    def rims_start(slot, src, dst):
        up, down = rim_copies(slot, src, dst)

        @pl.when(me_k > 0)
        def _():
            up.start()

        @pl.when(me_k < nk - 1)
        def _():
            down.start()

    def rims_wait(slot, src, dst):
        up, down = rim_copies(slot, src, dst)

        @pl.when(me_k > 0)
        def _():
            down.wait_recv()
            up.wait_send()

        @pl.when(me_k < nk - 1)
        def _():
            up.wait_recv()
            down.wait_send()

    def pack_row(ref, l, lane0):
        if W[l] >= 128:
            return jnp.concatenate(
                [ref[:, lane0 + 128 * i : lane0 + 128 * i + 128] for i in range(W[l] // 128)], axis=0
            )
        group = 128 // W[l]
        rows = C[l] // group
        base, shift = lane0 // 128 * 128, lane0 % 128
        out = None
        for g in range(group):
            v = ref[g * rows : (g + 1) * rows, base : base + 128]
            turn = (g * W[l] - shift) % 128
            v = pltpu.roll(v, turn, 1) if turn else v
            out = v if out is None else jnp.where(lane128 >= g * W[l], v, out)
        return out

    def unpack_row(ref, l, lane0, q):
        if W[l] >= 128:
            for i in range(W[l] // 128):
                ref[:, lane0 + 128 * i : lane0 + 128 * i + 128] = q[i * C[l] : (i + 1) * C[l]]
            return
        group = 128 // W[l]
        rows = C[l] // group
        base, shift = lane0 // 128 * 128, lane0 % 128
        here = (lane128 >= shift) & (lane128 < shift + W[l])
        for g in range(group):
            turn = (shift - g * W[l]) % 128
            v = pltpu.roll(q, turn, 1) if turn else q
            old = ref[g * rows : (g + 1) * rows, base : base + 128]
            ref[g * rows : (g + 1) * rows, base : base + 128] = jnp.where(here, v, old)

    def pack_rims(slot, arrays):
        for l in range(LEVELS):
            at = slice(sz.rim_off[l], sz.rim_off[l] + sz.rim_rows[l])
            rim_s[0, at, :] = pack_row(arrays[l], l, W[l]).astype(BF16)
            rim_s[1, at, :] = pack_row(arrays[l], l, N[l]).astype(BF16)

    def unpack_rims(slot, arrays):
        for l in range(LEVELS):
            at = slice(sz.rim_off[l], sz.rim_off[l] + sz.rim_rows[l])
            unpack_row(arrays[l], l, 0, rim_r[slot, 0, at, :].astype(F32))
            unpack_row(arrays[l], l, W[l] + N[l], rim_r[slot, 1, at, :].astype(F32))

    def each(l, body):
        rc, lanes = sz.chunk[l]

        def step(i, _):
            body(pl.multiple_of(i * rc, rc), rc, lanes)
            return 0

        lax.fori_loop(0, C[l] // rc, step, 0)

    def lane_chunks(l, lanes):
        return [(i, i + lanes) for i in range(0, NP[l], lanes)]

    def stack_columns(ref, l, r0, rc, a, b, v, back=False):
        lanes = b - a
        at = lax.broadcasted_iota(jnp.int32, (1, lanes), 1) & (W[l] - 1)
        left = jnp.where(at == 0, 0.0, pltpu.roll(v, 1, 1))
        right = jnp.where(at == W[l] - 1, 0.0, pltpu.roll(v, lanes - 1, 1))
        for u, part in enumerate((right, v, left) if back else (left, v, right)):
            ref[pl.ds(pl.multiple_of(u * C[l] + r0, 16), rc), a:b] = part.astype(BF16)

    def stack_rows(ref, l, r0, rc, v):
        for t in range(3):
            turn = ((t - 1) * W[l]) % NP[l]
            part = pltpu.roll(v, turn, 1) if turn else v
            ref[pl.ds(pl.multiple_of(t * C[l] + r0, 16), rc), :] = part.astype(BF16)

    def conv(l, w, which, src, dst, sign=1):
        c = C[l]
        if W[l] % 128 == 0:
            span = min(1024, N[l])

            def step(i, _):
                acc = None
                for t in range(3):
                    at = pl.ds(pl.multiple_of(i * span + (1 + sign * (t - 1)) * W[l], 128), span)
                    part = jnp.dot(
                        w[l][which, t * c : (t + 1) * c, :], src[l][:, at], preferred_element_type=F32
                    )
                    acc = part if acc is None else acc + part
                dst[l][:, pl.ds(pl.multiple_of(i * span + W[l], 128), span)] = acc
                return 0

            lax.fori_loop(0, N[l] // span, step, 0)
        else:
            rows = 96

            def step(i, _):
                acc = None
                for t in range(3):
                    at = pl.ds(pl.multiple_of(t * c + i * rows, 16), rows)
                    part = jnp.dot(w[l][which, at, :], src[l][...], preferred_element_type=F32)
                    turn = (sign * (1 - t) * W[l]) % NP[l]
                    part = pltpu.roll(part, turn, 1) if turn else part
                    acc = part if acc is None else acc + part
                dst[l][pl.ds(pl.multiple_of(i * rows, 16), rows), :] = acc
                return 0

            lax.fori_loop(0, c // rows, step, 0)

    def kernel_grad(l, src):
        c = C[l]
        if W[l] % 128 == 0:
            for t in range(3):
                kg[t * c : (t + 1) * c, 0 : 3 * c] = lax.dot_general(
                    g3[l][c : 2 * c, W[l] : W[l] + N[l]],
                    src[l][:, t * W[l] : t * W[l] + N[l]],
                    (((1,), (1,)), ((), ())),
                    preferred_element_type=F32,
                )
            return
        span = 96

        def step(i, _):
            at = pl.ds(pl.multiple_of(i * span, 16), span)
            kg[at, 0 : 3 * c] = lax.dot_general(
                t3[l][at, :], src[l][...], (((1,), (1,)), ((), ())), preferred_element_type=F32
            )
            return 0

        lax.fori_loop(0, 3 * c // span, step, 0)

    nc, ny, nx, nz = sz.nc, sz.ny, sz.nx, sz.nz
    my_core, my_y = lax.rem(me_b, nc), lax.div(me_b, nc)
    my_x, my_z = lax.rem(me_k, nx), lax.div(me_k, nx)

    def others(n, me):
        return [lax.rem(me + j, n) for j in range(1, n)]

    def remote(src, dst, send, recv, target):
        return pltpu.make_async_remote_copy(
            src_ref=src, dst_ref=dst, send_sem=send, recv_sem=recv, device_id=target, device_id_type=MESH
        )

    def sum_pack(c, l):
        n = C[l] // nb
        for q in range(nb):
            dst = part_a.at[c, q % nc, q // nc]
            for i in range(-(-3 * C[l] // 128)):
                at, rows = sz.spots[l, i]
                lanes = slice(128 * i, 128 * i + 128)
                parts = [kg[t * C[l] + q * n : t * C[l] + q * n + n, lanes] for t in range(3)]
                if rows > 3 * n:
                    parts.append(jnp.zeros((rows - 3 * n, 128), F32))
                dst[at : at + rows, :] = jnp.concatenate(parts, axis=0).astype(BF16)

    def sum_pack_unites():
        n = sz.uchan // nb
        for q in range(nb):
            dst = part_a.at[1, q % nc, q // nc]
            for j in range(3):
                for i in range(-(-C[j + 1] // 128)):
                    at, rows = sz.spots["u", j, i]
                    v = gun[j][q * n : q * n + n, 128 * i : 128 * i + 128]
                    if rows > n:
                        v = jnp.concatenate([v, jnp.zeros((rows - n, 128), F32)], axis=0)
                    dst[at : at + rows, :] = v.astype(BF16)

    def core_copies(c):
        out = []
        for other in others(nc, my_core):
            target = (my_y * nc + other, me_k)
            out.append(remote(part_a.at[c, other], got_a.at[c], ra_send.at[c], ra_recv.at[c], target))
        return out

    def y_copies(c, sending):
        out = []
        for other in others(ny, my_y):
            target = (other * nc + my_core, me_k)
            if sending:
                src, dst, sem = part_a.at[c, my_core, other], got_b.at[c, my_y], rb_recv.at[c, my_y]
            else:
                src, dst, sem = part_a.at[c, my_core, other], got_b.at[c, other], rb_recv.at[c, other]
            out.append(remote(src, dst, rb_send.at[c, other], sem, target))
        return out

    def row_copies(c, sending):
        out = []
        for other in others(nk, me_k):
            slot = me_k if sending else other
            out.append(
                remote(
                    part_a.at[c, my_core, my_y, pl.ds(pl.multiple_of(other * sz.part, 16), sz.part), :],
                    got_c.at[c, slot], rc_send.at[c, other], rc_recv.at[c, slot], (me_b, other)
                )
            )
        return out

    def back_copies(c, sending):
        out = []
        for other in others(nk, me_k):
            slot = me_k if sending else other
            out.append(
                remote(
                    got_d.at[c, me_k], got_d.at[c, slot], rd_send.at[c, other], rd_recv.at[c, slot], (me_b, other)
                )
            )
        return out

    def finish(pair):
        sent, received = pair
        for copy in received:
            copy.wait_recv()
        for copy in sent:
            copy.wait_send()

    def sum_first(c, src):
        for l in sz.sum_levels:
            kernel_grad(l, src)
            sum_pack(c, l)
        if c == 1:
            sum_pack_unites()
        for copy in core_copies(c):
            copy.start()

    def sum_second(c):
        copies = core_copies(c)
        finish((copies, copies))
        for y in range(ny):
            v = part_a[c, my_core, y].astype(F32)
            if nc > 1:
                v = v + got_a[c, y].astype(F32)
            part_a[c, my_core, y] = v.astype(BF16)
        for copy in y_copies(c, True):
            copy.start()

    def sum_third(c):
        finish((y_copies(c, True), y_copies(c, False)))
        got_b[c, my_y] = part_a[c, my_core, my_y]
        for k in range(nk):
            at = slice(k * sz.part, (k + 1) * sz.part)
            v = got_b[c, 0, at, :].astype(F32)
            for y in range(1, ny):
                v = v + got_b[c, y, at, :].astype(F32)
            part_a[c, my_core, my_y, at, :] = v.astype(BF16)
        for copy in row_copies(c, True):
            copy.start()

    def sum_fourth(c):
        finish((row_copies(c, True), row_copies(c, False)))
        mine = pl.ds(pl.multiple_of(me_k * sz.part, 16), sz.part)
        got_c[c, me_k] = part_a[c, my_core, my_y, mine, :]
        v = got_c[c, 0].astype(F32)
        for k in range(1, nk):
            v = v + got_c[c, k].astype(F32)
        got_d[c, me_k] = v.astype(BF16)
        for copy in back_copies(c, True):
            copy.start()

    def sum_last(c):
        finish((back_copies(c, True), back_copies(c, False)))
        pltpu.make_async_copy(got_d.at[c], sums_ref.at[c], out_sem.at[c]).start()

    c3 = C[3] // nb
    half = c3 // 2

    def pack_pixels(ref):
        parts = []
        for q in range(nb):
            at = C[3] + q * c3
            low = pltpu.roll(ref[at : at + half, :].astype(F32), 128 - W[3], 1)
            high = pltpu.roll(ref[at + half : at + c3, :].astype(F32), 64 - W[3], 1)
            parts.append(jnp.where(lane128 < 64, low, high))
        return jnp.concatenate(parts, axis=0).astype(BF16)

    def unpack_pixels(first, second):
        first, second = first.astype(F32), second.astype(F32)
        low = jnp.where(lane128 < 64, first, pltpu.roll(second, 64, 1))
        high = jnp.where(lane128 < 64, pltpu.roll(first, 64, 1), second)
        return low, high

    def gather_copies(c, step, sending):
        if not sz.gather:
            return []
        n, me = ((nz, my_z), (nx, my_x), (ny, my_y), (nc, my_core))[step]
        out = []
        for other in others(n, me):
            slot = me if sending else other
            if step == 0:
                ref, target = xg.at[c, my_core, my_y, my_x, slot], (me_b, other * nx + my_x)
            elif step == 1:
                ref, target = xg.at[c, my_core, my_y, slot], (me_b, my_z * nx + other)
            elif step == 2:
                ref, target = xg.at[c, my_core, slot], (other * nc + my_core, me_k)
            else:
                ref, target = xg.at[c, slot], (my_y * nc + other, me_k)
            out.append(remote(ref, ref, xg_send.at[c, step, other], xg_recv.at[c, step, slot], target))
        return out

    def gather_start(c, step):
        for copy in gather_copies(c, step, True):
            copy.start()

    def gather_wait(c, step):
        finish((gather_copies(c, step, True), gather_copies(c, step, False)))

    def gather_begin(c, ref):
        if sz.gather:
            xg[c, my_core, my_y, my_x, my_z] = pack_pixels(ref[3])
            gather_start(c, 0)

    def gather_next(c, step):
        gather_wait(c, step)
        gather_start(c, step + 1)

    def grad_copies(c, step, sending):
        out = []
        if step == 0:
            for other in others(nb, me_b):
                slot = me_b if sending else other
                src = gs.at[c, other]
                out.append(
                    remote(src, gr.at[c, me_k, slot], g1_send.at[c, other], g1_recv.at[c, slot], (other, me_k))
                )
        else:
            for other in others(nk, me_k):
                slot = me_k if sending else other
                ref = gr.at[c, slot]
                out.append(remote(gr.at[c, me_k], ref, g2_send.at[c, other], g2_recv.at[c, slot], (me_b, other)))
        return out

    def grad_begin(c):
        if sz.gather:
            v = pack_pixels(g3[3])
            for q in range(nb):
                gs[c, q] = v[q * half : (q + 1) * half]
            for copy in grad_copies(c, 0, True):
                copy.start()

    def grad_next(c):
        if sz.gather:
            finish((grad_copies(c, 0, True), grad_copies(c, 0, False)))
            gr[c, me_k, me_b] = gs[c, me_b]
            for copy in grad_copies(c, 1, True):
                copy.start()

    image = nz * 128

    def coarse_inputs(c):
        if not sz.gather:
            return
        gather_wait(c, 3)
        at = lane128 & (W[3] - 1)

        def item(b, _):
            def group(q, _):
                for z in range(nz):
                    rows = pl.ds(pl.multiple_of(q * half, 16), half)
                    core, y = lax.rem(b, nc), lax.div(b, nc)
                    pair = unpack_pixels(xg[c, core, y, 0, z, rows, :], xg[c, core, y, 1, z, rows, :])
                    for i, v in enumerate(pair):
                        left = jnp.where(at == 0, 0.0, pltpu.roll(v, 1, 1))
                        right = jnp.where(at == W[3] - 1, 0.0, pltpu.roll(v, 127, 1))
                        for u, part in enumerate((left, v, right)):
                            spot = pl.ds(pl.multiple_of(u * C[3] + q * c3 + i * half, 16), half)
                            x3g[b, spot, 128 * z : 128 * z + 128] = part.astype(BF16)
                return 0

            lax.fori_loop(0, nb, group, 0)
            return 0

        lax.fori_loop(0, nb, item, 0)

    def coarse_copy(c, i):
        at = pl.ds(i * c3 if isinstance(i, int) else pl.multiple_of(i * c3, 16), c3)
        slot = i % 2 if isinstance(i, int) else lax.rem(i, 2)
        return pltpu.make_async_copy(cstage.at[slot], coarse_ref.at[c, at, :], cstage_sem.at[slot])

    def coarse_local(c, src):
        def step(i, _):
            at = pl.ds(pl.multiple_of(i * c3, 16), c3)
            cstage[0] = lax.dot_general(
                t3[3][at, :], src[3][...], (((1,), (1,)), ((), ())), preferred_element_type=F32
            )
            copy = pltpu.make_async_copy(cstage.at[0], coarse_ref.at[c, at, :], cstage_sem.at[0])
            copy.start()
            copy.wait()
            return 0

        lax.fori_loop(0, 3 * nb, step, 0)

    def coarse_gradient(c):
        if not sz.gather:
            coarse_local(c, a3 if c else x3)
            return
        finish((grad_copies(c, 1, True), grad_copies(c, 1, False)))
        lane = lax.broadcasted_iota(jnp.int32, (1, image), 1)

        def item(b, _):
            low, high = [], []
            for z in range(nz):
                first, second = unpack_pixels(gr[c, nx * z, b], gr[c, nx * z + 1, b])
                low.append(first)
                high.append(second)
            for i, parts in enumerate((low, high)):
                v = jnp.concatenate(parts, axis=1) if nz > 1 else parts[0]
                up_ = jnp.where(lane >= image - W[3], 0.0, pltpu.roll(v, image - W[3], 1))
                down = jnp.where(lane < W[3], 0.0, pltpu.roll(v, W[3], 1))
                for t, part in enumerate((up_, v, down)):
                    spot = t * c3 + i * half
                    t3g[b, spot : spot + half, :] = part.astype(BF16)
            return 0

        lax.fori_loop(0, nb, item, 0)

        def step(i, _):
            at = pl.ds(pl.multiple_of(i * c3, 16), c3)
            acc = None
            for b in range(nb):
                part = lax.dot_general(
                    t3g[b, at, :], x3g[b, :, 0:image], (((1,), (1,)), ((), ())), preferred_element_type=F32
                )
                acc = part if acc is None else acc + part
            slot = lax.rem(i, 2)

            @pl.when(i >= 2)
            def _():
                coarse_copy(c, i - 2).wait()

            cstage[slot] = acc
            coarse_copy(c, i).start()
            return 0

        lax.fori_loop(0, 3, step, 0)
        coarse_copy(c, 1).wait()
        coarse_copy(c, 2).wait()

    def moments(arrays):
        for l in range(LEVELS):

            def body(r0, rc, lanes, l=l):
                acc = jnp.zeros((rc, 128), F32)
                for a, b in lane_chunks(l, lanes):
                    m = masks[l][1:2, a:b] > 0
                    acc = acc + fold(jnp.where(m, arrays[l][pl.ds(r0, rc), a:b], 0.0))
                stat_a[pl.ds(pl.multiple_of(OFF[l] + r0, 16), rc), :] = acc

            each(l, body)
        for l in range(LEVELS):
            at = slice(OFF[l], OFF[l] + C[l])
            s = jnp.sum(stat_a[at, :], axis=1, keepdims=True) * inv_local[l]
            cols[LOCAL, at, :] = jnp.broadcast_to(s, (C[l], 128))
        for l in range(LEVELS):

            def body(r0, rc, lanes, l=l):
                acc = jnp.zeros((rc, 128), F32)
                mean = col(LOCAL, l, r0, rc, lanes)
                for a, b in lane_chunks(l, lanes):
                    m = masks[l][1:2, a:b] > 0
                    d = jnp.where(m, arrays[l][pl.ds(r0, rc), a:b] - mean, 0.0)
                    acc = acc + fold(d * d)
                stat_b[pl.ds(pl.multiple_of(OFF[l] + r0, 16), rc), :] = acc

            each(l, body)
        return record(stat_a, stat_b, sz.blocks)

    def halves(l):
        return max(1, W[l] // 128)

    def to_stage(ref, src):
        for h in range(src.shape[1] // 128):
            ref[h] = src[:, 128 * h : 128 * h + 128].astype(F32)

    for l in range(LEVELS):
        if W[l] >= 128:
            to_stage(stage, feats[l])
            for r in range(R[l]):
                for h in range(halves(l)):
                    a = (r + 1) * W[l] + 128 * h
                    xf[l][:, a : a + 128] = stage[h, pl.ds(r, C[l], stride=R[l]), :]
        else:
            v = feats[l][...].astype(F32)
            v = jnp.concatenate([v, jnp.zeros((NP[l] - N[l], C[l]), F32)], axis=0)
            xf[l][...] = pltpu.roll(v.T, W[l], 1)
    pack_rims(0, xf)
    rims_start(0, rim_s, rim_r.at[0])
    to_stage(stage, ograd)
    widen(0)
    rims_wait(0, rim_s, rim_r.at[0])
    unpack_rims(0, xf)
    for l in range(LEVELS):

        def body(r0, rc, lanes, l=l):
            for a, b in lane_chunks(l, lanes):
                m = masks[l][0:1, a:b] > 0
                stack_columns(x3[l], l, r0, rc, a, b, jnp.where(m, xf[l][pl.ds(r0, rc), a:b], 0.0))

        each(l, body)

    gather_begin(0, x3)
    for l in range(LEVELS):
        conv(l, wide, 0, x3, y1)
    pack_rims(1, y1)
    rims_start(1, rim_s, rim_r.at[1])

    def while_first():
        gather_next(0, 0)
        turn(0)

    got = gather_moments(0, moments(y1), n_a, n_b, (while_first, lambda: widen(1)))
    rims_wait(1, rim_s, rim_r.at[1])
    mean1_p = got[0:8] * inv_count
    rstd1_p = lax.rsqrt(got[8:16] * inv_count + EPSILON)
    to_columns([mean1_p, rstd1_p], cols, [MEAN, RSTD], sz.blocks)
    unpack_rims(1, y1)

    def pre_of(hat, gain, shift, l, r0, rc, lanes):
        return hat * col(gain, l, r0, rc, lanes) + col(shift, l, r0, rc, lanes)

    for l in range(LEVELS):

        def body(r0, rc, lanes, l=l):
            for a, b in lane_chunks(l, lanes):
                m = masks[l][0:1, a:b] > 0
                hat = (y1[l][pl.ds(r0, rc), a:b] - col(MEAN, l, r0, rc, lanes)) * col(RSTD, l, r0, rc, lanes)
                y1[l][pl.ds(r0, rc), a:b] = hat
                pre = pre_of(hat, GAIN1, SHIFT1, l, r0, rc, lanes)
                stack_columns(a3[l], l, r0, rc, a, b, jnp.where(m, pre * sigmoid(pre), 0.0))

        each(l, body)

    gather_begin(1, a3)
    for l in range(LEVELS):
        conv(l, wide, 1, a3, y2)
    pack_rims(2, y2)
    rims_start(2, rim_s, rim_r.at[2])

    def while_second():
        gather_next(0, 1)
        gather_next(1, 0)

    got = gather_moments(1, moments(y2), n_a, n_b, (while_second, lambda: turn(1)))
    rims_wait(2, rim_s, rim_r.at[2])
    mean2_p = got[0:8] * inv_count
    rstd2_p = lax.rsqrt(got[8:16] * inv_count + EPSILON)
    to_columns([mean2_p, rstd2_p], cols, [MEAN, RSTD], sz.blocks)
    unpack_rims(2, y2)

    def start_part(l, r0, rc, a, b):
        return x3[l][pl.ds(pl.multiple_of(C[l] + r0, 16), rc), a:b].astype(F32)

    for l in range(LEVELS):

        def body(r0, rc, lanes, l=l):
            for a, b in lane_chunks(l, lanes):
                m = masks[l][0:1, a:b] > 0
                hat = (y2[l][pl.ds(r0, rc), a:b] - col(MEAN, l, r0, rc, lanes)) * col(RSTD, l, r0, rc, lanes)
                y2[l][pl.ds(r0, rc), a:b] = hat
                pre = pre_of(hat, GAIN2, SHIFT2, l, r0, rc, lanes)
                pre = jnp.where(m, pre, 0.0) + start_part(l, r0, rc, a, b)
                p1[l][pl.ds(r0, rc), a:b] = pre
                if l:
                    br[l - 1][pl.ds(r0, rc), a:b] = (pre * sigmoid(pre)).astype(BF16)

        each(l, body)

    UC_ = sz.uchan
    for j in range(3):
        l = j + 1
        uo[j][...] = jnp.dot(unites[j][...], br[j][...], preferred_element_type=F32)
    for j in range(3):
        l = j + 1
        m = masks[l][1:2, :] > 0
        v = jnp.where(m, uo[j][...], 0.0)
        part = fold(v)
        ustat_a[j * UC_ : (j + 1) * UC_, :] = part
        mean = jnp.sum(part, axis=1, keepdims=True) * inv_local[l]
        d = jnp.where(m, uo[j][...] - mean, 0.0)
        ustat_b[j * UC_ : (j + 1) * UC_, :] = fold(d * d)

    def while_unite():
        gather_next(0, 2)
        gather_next(1, 1)

    got = gather_moments(2, record(ustat_a, ustat_b, sz.ublocks), un_a, un_b, (while_unite, None))
    umean_p = got[0:8] * inv_ucount
    urstd_p = lax.rsqrt(got[8:16] * inv_ucount + EPSILON)
    to_columns([umean_p, urstd_p], ucols, [UMEAN, URSTD], sz.ublocks)

    at_top = me_k == 0
    at_bottom = me_k == nk - 1
    fine = W[0]
    split = lambda v: (v.astype(BF16), (v - v.astype(BF16).astype(F32)).astype(BF16))

    def edge(l, n):
        lane = lax.broadcasted_iota(jnp.int32, (1, n), 1)
        return lane

    for j in range(3):
        l = j + 1
        m = masks[l][0:1, :] > 0
        hat = (uo[j][...] - ucol(UMEAN, j, NP[l])) * ucol(URSTD, j, NP[l])
        uo[j][...] = hat
        norm = jnp.where(m, hat * ucol(UGAIN, j, NP[l]) + ucol(USHIFT, j, NP[l]), 0.0)
        lane = edge(l, NP[l])
        norm = jnp.where((lane < W[l]) & at_top, pltpu.roll(norm, NP[l] - W[l], 1), norm)
        norm = jnp.where((lane >= W[l] + N[l]) & at_bottom, pltpu.roll(norm, W[l], 1), norm)
        hi, lo = split(norm)
        both = jnp.concatenate([hi, lo], axis=0)
        span = max(128, W[l])
        width = tables[j].shape[1]
        for i in range(NP[l] // span):
            broad = jnp.dot(both[:, span * i : span * i + span], tables[j][...], preferred_element_type=F32)
            up[j][:, width * i : width * i + width] = broad[0:UC_] + broad[UC_:]

    blends = [blend(2 ** (j + 1), R[0]) for j in range(3)]

    def total_body(r0, rc, lanes):
        rows = pl.ds(r0, rc)
        coarse = [{}, {}, {}]
        have = [{}, {}, {}]
        for g in range(R[0]):
            a, b = (g + 1) * fine, (g + 2) * fine
            pre = p1[0][rows, a:b]
            total = pre * sigmoid(pre)
            for j in range(3):
                low, frac = blends[j][g]
                for i in (low, low + 1):
                    if i not in have[j]:
                        have[j][i] = up[j][rows, i * fine : (i + 1) * fine]
                total = total + ((1.0 - frac) * have[j][low] + frac * have[j][low + 1])
            m = masks[0][1:2, a:b] > 0
            sig = sigmoid(total)
            out = jnp.where(m, total * sig, 0.0)
            slope = sig * (1.0 + total * (1.0 - sig))
            spots = [(h, pl.ds(r0 * R[0] + g, rc, stride=R[0])) for h in range(halves(0))]
            grad = jnp.concatenate([stage[h, at, :] for h, at in spots], axis=1)
            grad = jnp.where(m, grad * slope, 0.0)
            for h, at in spots:
                stage[h, at, :] = out[:, 128 * h : 128 * h + 128]
            xf[0][rows, a:b] = grad
            for j in range(3):
                low, frac = blends[j][g]
                for i, weight in ((low, 1.0 - frac), (low + 1, frac)):
                    coarse[j][i] = weight * grad if i not in coarse[j] else coarse[j][i] + weight * grad
                done = [i for i in coarse[j] if g + 1 == R[0] or i < blends[j][g + 1][0]]
                for i in done:
                    up[j][rows, i * fine : (i + 1) * fine] = coarse[j].pop(i)

    def total_step(i, _):
        total_body(pl.multiple_of(i * 16, 16), 16, fine)
        return 0

    lax.fori_loop(0, UC_ // 16, total_step, 0)
    for h in range(halves(0)):
        united_ref[:, 128 * h : 128 * h + 128] = stage[h].astype(BF16)

    ud = []
    for j in range(3):
        l = j + 1
        span = max(128, W[l])
        width = tables[j].shape[1]
        parts = []
        for i in range(NP[l] // span):
            hi, lo = split(up[j][:, width * i : width * i + width])
            both = jnp.concatenate([hi, lo], axis=0)
            narrow = jnp.dot(both, tables_t[j][...], preferred_element_type=F32)
            parts.append(narrow[0:UC_] + narrow[UC_:])
        d = parts[0] if len(parts) == 1 else jnp.concatenate(parts, axis=1)
        lane = edge(l, NP[l])
        fold_top = jnp.where((lane >= W[l]) & (lane < 2 * W[l]) & at_top, pltpu.roll(d, W[l], 1), 0.0)
        fold_bottom = jnp.where(
            (lane >= N[l]) & (lane < W[l] + N[l]) & at_bottom, pltpu.roll(d, NP[l] - W[l], 1), 0.0
        )
        d = d + fold_top + fold_bottom
        d = jnp.where(masks[l][0:1, :] > 0, d, 0.0)
        ustat_a[j * UC_ : (j + 1) * UC_, :] = fold(d * uo[j][...])
        ustat_b[j * UC_ : (j + 1) * UC_, :] = fold(d)
        up[j][:, 0 : NP[l]] = d
    at = 0
    lay = []
    for j in range(3):
        l = j + 1
        n = max(2 * W[l], 128)
        lay.append((at, n))
        mid_s[0, :, at : at + n] = up[j][:, 0:n].astype(BF16)
        mid_s[1, :, at : at + n] = up[j][:, NP[l] - n : NP[l]].astype(BF16)
        at += n
    mid_s[0, :, at : at + fine] = xf[0][:, fine : 2 * fine].astype(BF16)
    mid_s[1, :, at : at + fine] = xf[0][:, N[0] : N[0] + fine].astype(BF16)
    rims_start(3, mid_s, mid_r)
    got4 = gather_sums(3, record(ustat_a, ustat_b, sz.ublocks), (lambda: gather_next(1, 2), None))
    totals_ref[0] = got4
    rims_wait(3, mid_s, mid_r)
    scale_p = urstd_p * ugain_p
    to_columns(
        [scale_p, got4[8:16] * inv_ucount, got4[0:8] * inv_ucount], ucols, [UA, UB, UC], sz.ublocks
    )
    xf[0][:, 0:fine] = mid_r[0, :, at : at + fine].astype(F32)
    xf[0][:, N[0] + fine : NP[0]] = mid_r[1, :, at : at + fine].astype(F32)
    for j in range(3):
        l = j + 1
        start, n = lay[j]
        lane = edge(l, n)
        above = mid_r[0, :, start : start + n].astype(F32)
        below = mid_r[1, :, start : start + n].astype(F32)
        if NP[l] == n:
            above, below = pltpu.roll(above, n // 2, 1), pltpu.roll(below, n // 2, 1)
            d = up[j][:, 0:n]
            d = d + jnp.where((lane < 2 * W[l]) & (me_k > 0), above, 0.0)
            d = d + jnp.where((lane >= n - 2 * W[l]) & (me_k < nk - 1), below, 0.0)
            up[j][:, 0:n] = d
        else:
            up[j][:, 0:n] = up[j][:, 0:n] + jnp.where((lane >= 0) & (me_k > 0), above, 0.0)
            up[j][:, NP[l] - n : NP[l]] = up[j][:, NP[l] - n : NP[l]] + jnp.where(
                (lane >= 0) & (me_k < nk - 1), below, 0.0
            )
    for j in range(3):
        l = j + 1
        d = up[j][:, 0 : NP[l]]
        g = ucol(UA, j, NP[l]) * (d - ucol(UB, j, NP[l]) - uo[j][...] * ucol(UC, j, NP[l]))
        g = jnp.where(masks[l][0:1, :] > 0, g, 0.0)
        low = g.astype(BF16)
        xf[l][...] = jnp.dot(unites[j][...].T, low, preferred_element_type=F32)
        own = jnp.where(masks[l][1:2, :] > 0, g, 0.0).astype(BF16)
        gun[j][:, 0 : C[l]] = lax.dot_general(
            own, br[j][...], (((1,), (1,)), ((), ())), preferred_element_type=F32
        )

    for l in range(LEVELS):

        def body(r0, rc, lanes, l=l):
            acc_g = jnp.zeros((rc, 128), F32)
            acc_s = jnp.zeros((rc, 128), F32)
            for a, b in lane_chunks(l, lanes):
                m = masks[l][1:2, a:b] > 0
                pre = p1[l][pl.ds(r0, rc), a:b]
                sig = sigmoid(pre)
                d = xf[l][pl.ds(r0, rc), a:b] * (sig * (1.0 + pre * (1.0 - sig)))
                xf[l][pl.ds(r0, rc), a:b] = d
                d = jnp.where(m, d, 0.0)
                acc_s = acc_s + fold(d)
                acc_g = acc_g + fold(jnp.where(m, d * y2[l][pl.ds(r0, rc), a:b], 0.0))
            at = pl.ds(pl.multiple_of(OFF[l] + r0, 16), rc)
            stat_a[at, :] = acc_g
            stat_b[at, :] = acc_s

        each(l, body)
    got5 = gather_sums(4, record(stat_a, stat_b, sz.blocks), (lambda: coarse_inputs(1), None))
    totals_ref[1] = got5
    to_columns(
        [rstd2_p * gain2_p, got5[8:16] * inv_count, got5[0:8] * inv_count], cols, [CA, CB, CC], sz.blocks
    )

    def store_gradient(l, r0, rc, parts):
        v = parts[0] if len(parts) == 1 else jnp.concatenate(parts, axis=1)
        if l not in sz.stacked:
            return
        stack_rows(t3[l], l, r0, rc, jnp.where(masks[l][1:2, :] > 0, v, 0.0))

    for l in range(LEVELS):

        def body(r0, rc, lanes, l=l):
            parts = []
            for a, b in lane_chunks(l, lanes):
                m = masks[l][0:1, a:b] > 0
                hat = y2[l][pl.ds(r0, rc), a:b]
                d = xf[l][pl.ds(r0, rc), a:b]
                g = col(CA, l, r0, rc, lanes) * (
                    d - col(CB, l, r0, rc, lanes) - hat * col(CC, l, r0, rc, lanes)
                )
                g = jnp.where(m, g, 0.0)
                stack_columns(g3[l], l, r0, rc, a, b, g, back=True)
                parts.append(g)
            store_gradient(l, r0, rc, parts)

        each(l, body)

    grad_begin(1)

    for l in range(LEVELS):
        conv(l, wide, 1, g3, p1, -1)
    for l in range(LEVELS):

        def body(r0, rc, lanes, l=l):
            acc_g = jnp.zeros((rc, 128), F32)
            acc_s = jnp.zeros((rc, 128), F32)
            for a, b in lane_chunks(l, lanes):
                m = masks[l][1:2, a:b] > 0
                hat = y1[l][pl.ds(r0, rc), a:b]
                pre = pre_of(hat, GAIN1, SHIFT1, l, r0, rc, lanes)
                sig = sigmoid(pre)
                d = p1[l][pl.ds(r0, rc), a:b] * (sig * (1.0 + pre * (1.0 - sig)))
                d = jnp.where(m, d, 0.0)
                p1[l][pl.ds(r0, rc), a:b] = d
                acc_s = acc_s + fold(d)
                acc_g = acc_g + fold(jnp.where(m, d * hat, 0.0))
            at = pl.ds(pl.multiple_of(OFF[l] + r0, 16), rc)
            stat_a[at, :] = acc_g
            stat_b[at, :] = acc_s

        each(l, body)
    pack_rims(3, p1)
    rims_start(4, rim_s, rim_r.at[3])

    def while_back():
        grad_next(1)
        sum_first(1, a3)

    def while_back_rows():
        coarse_gradient(1)
        coarse_inputs(0)

    got6 = gather_sums(5, record(stat_a, stat_b, sz.blocks), (while_back, while_back_rows))
    totals_ref[2] = got6
    rims_wait(4, rim_s, rim_r.at[3])
    to_columns(
        [rstd1_p * gain1_p, got6[8:16] * inv_count, got6[0:8] * inv_count], cols, [CA, CB, CC], sz.blocks
    )
    unpack_rims(3, p1)
    for l in (3, 0, 1, 2):

        def body(r0, rc, lanes, l=l):
            parts = []
            for a, b in lane_chunks(l, lanes):
                m = masks[l][0:1, a:b] > 0
                hat = y1[l][pl.ds(r0, rc), a:b]
                d = p1[l][pl.ds(r0, rc), a:b]
                g = col(CA, l, r0, rc, lanes) * (
                    d - col(CB, l, r0, rc, lanes) - hat * col(CC, l, r0, rc, lanes)
                )
                g = jnp.where(m, g, 0.0)
                stack_columns(g3[l], l, r0, rc, a, b, g, back=True)
                parts.append(g)
            store_gradient(l, r0, rc, parts)

        each(l, body)
        if l == 3:
            grad_begin(0)

    sum_first(0, x3)
    sum_second(1)
    grad_next(0)

    def features_out(l):
        if W[l] < 128:
            v = jnp.where(masks[l][1:2, :] > 0, y1[l][...] + xf[l][...], 0.0)
            gfeat[l][...] = pltpu.roll(v, NP[l] - W[l], 1).T[0 : N[l]].astype(BF16)
            return

        def body(r0, rc, lanes):
            for r in range(R[l]):
                for h in range(halves(l)):
                    a = (r + 1) * W[l] + 128 * h
                    m = masks[l][1:2, a : a + 128] > 0
                    v = y1[l][pl.ds(r0, rc), a : a + 128] + xf[l][pl.ds(r0, rc), a : a + 128]
                    stage[h, pl.ds(r0 * R[l] + r, rc, stride=R[l]), :] = jnp.where(m, v, 0.0)

        each(l, body)
        for h in range(halves(l)):
            gfeat[l][:, 128 * h : 128 * h + 128] = stage[h].astype(BF16)

    for l in (0, 1):
        conv(l, wide, 0, g3, y1, -1)
        features_out(l)
    sum_second(0)
    sum_third(1)
    for l in (2, 3):
        conv(l, wide, 0, g3, y1, -1)
        features_out(l)
    sum_fourth(1)
    sum_third(0)
    coarse_gradient(0)
    sum_fourth(0)
    sum_last(1)
    sum_last(0)
    for c in range(2):
        pltpu.make_async_copy(got_d.at[c], sums_ref.at[c], out_sem.at[c]).wait()


def last_kernel(sz, nb, *refs):
    it = iter(refs)
    take = lambda n: [next(it) for _ in range(n)]
    maps = take(5)
    sums, totals = take(2)
    (coarse,) = take(1)
    maps_out = take(5)
    kernels = take(4)
    unites = take(3)
    norm_gains, norm_shifts, unite_gains, unite_shifts = take(4)
    (sem,) = take(1)
    copies = [pltpu.make_async_copy(a, b, sem.at[i]) for i, (a, b) in enumerate(zip(maps, maps_out))]
    for copy in copies:
        copy.start()
    C = sz.chan
    for l in range(LEVELS):
        n = C[l] // nb
        for c in range(2):
            if l in sz.sum_levels:
                parts = []
                for i in range(-(-3 * C[l] // 128)):
                    at, rows = sz.spots[l, i]
                    parts.append(sums[c, at : at + rows, :].astype(F32))
                v = jnp.concatenate(parts, axis=1)
            for t in range(3):
                for u in range(3):
                    if l in sz.sum_levels:
                        kernels[l][c, t, u] = v[t * n : (t + 1) * n, u * C[l] : (u + 1) * C[l]]
                    else:
                        kernels[l][c, t, u] = coarse[c, t * n : (t + 1) * n, u * C[l] : (u + 1) * C[l]]
    n = sz.uchan // nb
    for j in range(3):
        width = C[j + 1]
        for i in range(-(-width // 128)):
            at, _ = sz.spots["u", j, i]
            m = min(128, width - 128 * i)
            unites[j][:, 128 * i : 128 * i + m] = sums[1, at : at + n, 0:m].astype(F32)
    for row, which in ((0, 2), (1, 1)):
        for k in range(sz.blocks):
            m = min(128, sz.total - 128 * k)
            for ref, base in ((norm_gains, 0), (norm_shifts, 8)):
                ref[row : row + 1, 128 * k : 128 * k + m] = totals[which, base + k : base + k + 1, 0:m]
    for ref, base in ((unite_gains, 0), (unite_shifts, 8)):
        v = jnp.concatenate([totals[0, base + k : base + k + 1, :] for k in range(sz.ublocks)], axis=1)
        for j in range(3):
            ref[j : j + 1, :] = v[:, j * sz.uchan : (j + 1) * sz.uchan]
    for copy in copies:
        copy.wait()


def body(*args):
    features = args[0:4]
    blocks = args[4:8]
    unites = args[8:11]
    norm_gains, norm_shifts, unite_gains, unite_shifts, output_grad, heights, widths, item_slot = args[11:]
    nb = lax.axis_size("batch")
    nk = lax.axis_size("rows")
    sz = Sizes(features, nb, nk)
    C, R, W, N, NP = sz.chan, sz.rows, sz.width, sz.own, sz.flat

    flat = [
        f.reshape(C[l] * R[l], W[l]) if W[l] >= 128 else f.transpose(0, 2, 3, 1).reshape(N[l], C[l])
        for l, f in enumerate(features)
    ]
    ograd = output_grad.reshape(C[0] * R[0], W[0])
    blocks = [b.reshape(2, 3, 3 * C[l], C[l]) for l, b in enumerate(blocks)]

    tables = [column_table(W[l], W[0]) for l in range(1, 4)]
    operands = [heights, widths, item_slot, *flat, ograd, *blocks, *unites]
    operands += [norm_gains, norm_shifts, unite_gains, unite_shifts]
    operands += [jnp.asarray(t, BF16) for t in tables] + [jnp.asarray(t.T, BF16) for t in tables]

    shape = jax.ShapeDtypeStruct
    map_shapes = [(C[0] * R[0], W[0])]
    map_shapes += [(C[l] * R[l], W[l]) if W[l] >= 128 else (N[l], C[l]) for l in range(4)]
    outs = [shape(m, BF16) for m in map_shapes]
    outs += [shape((2, nk, sz.part, 128), BF16)]
    outs += [shape((2, 3 * C[3] // nb if sz.gather else 3 * C[3], 3 * C[3]), F32)]
    outs += [shape((3, 16, 128), F32)]
    vm = pltpu.VMEM
    scratch = [
        vm((3, 3 * C[l], C[l]), BF16) for l in range(3 if sz.gather else 4)
    ]
    scratch += [vm((2, 3 * C[l], 3 * C[l]), BF16) for l in range(4)]
    scratch += [vm((max(1, W[0] // 128), C[0] * R[0], 128), F32)]
    for _ in range(3):
        scratch += [vm((3 * C[l], NP[l]), BF16) for l in range(4)]
    scratch += [vm((3 * C[l], NP[l]), BF16) for l in sz.stacked]
    scratch += [vm((2, C[3] // nb, 3 * C[3]), F32), pltpu.SemaphoreType.DMA((2,))]
    top = C[sz.sum_levels[-1]]
    scratch += [vm((3 * top, -(-3 * top // 128) * 128), F32)]
    scratch += [vm((sz.uchan, -(-C[l] // 128) * 128), F32) for l in range(1, 4)]
    for _ in range(4):
        scratch += [vm((C[l], NP[l]), F32) for l in range(4)]
    scratch += [vm((C[l], NP[l]), BF16) for l in range(1, 4)]
    scratch += [vm((sz.uchan, NP[l]), F32) for l in range(1, 4)]
    scratch += [vm((sz.uchan, (R[l] + 2) * W[0]), F32) for l in range(1, 4)]
    scratch += [
        vm((N_COLS, sz.blocks * 128, 128), F32),
        vm((N_UCOLS, sz.ublocks * 128, 128), F32),
        vm((sz.blocks * 128, 128), F32),
        vm((sz.blocks * 128, 128), F32),
        vm((sz.ublocks * 128, 128), F32),
        vm((sz.ublocks * 128, 128), F32),
        vm((nb, 8, 128), F32),
        vm((nk, 8, 128), F32),
        vm((nb, 8, 128), F32),
        vm((nk, 8, 128), F32),
    ]
    scratch += [vm((8, NP[l]), F32) for l in range(4)]
    mid = sum(max(2 * W[l], 128) for l in range(1, 4)) + W[0]
    scratch += [
        vm((6, nb, 16, 128), F32),
        vm((6, nk, 16, 128), F32),
        vm((2, sz.rim_total, 128), BF16),
        vm((4, 2, sz.rim_total, 128), BF16),
        vm((2, sz.uchan, mid), BF16),
        vm((2, sz.uchan, mid), BF16),
        pltpu.SemaphoreType.DMA((6, nb)),
        pltpu.SemaphoreType.DMA((6, nb)),
        pltpu.SemaphoreType.DMA((6, nk)),
        pltpu.SemaphoreType.DMA((6, nk)),
        pltpu.SemaphoreType.DMA((5, 2)),
        pltpu.SemaphoreType.DMA((5, 2)),
        pltpu.SemaphoreType.DMA((4, 2)),
        pltpu.SemaphoreType.DMA((2, 9)),
        vm((8, sz.blocks * 128), F32),
        vm((8, sz.ublocks * 128), F32),
        vm((2, sz.nc, sz.ny, sz.sum_rows, 128), BF16),
        vm((2, sz.ny, sz.sum_rows, 128), BF16),
        vm((2, sz.ny, sz.sum_rows, 128), BF16),
        vm((2, nk, sz.part, 128), BF16),
        vm((2, nk, sz.part, 128), BF16),
        pltpu.SemaphoreType.DMA((2,)),
    ]
    sems = pltpu.SemaphoreType.DMA
    scratch += [sems((2,)), sems((2,))] + [sems((2, sz.ny))] * 2 + [sems((2, nk))] * 4
    if sz.gather:
        half = C[3] // nb // 2
        most = max(sz.nz, sz.nx, sz.ny, sz.nc)
        scratch += [
            vm((2, sz.nc, sz.ny, sz.nx, sz.nz, C[3] // 2, 128), BF16),
            vm((2, nb, half, 128), BF16),
            vm((2, nk, nb, half, 128), BF16),
            vm((max(3, nb), 3 * C[3], max(C[3], 128 * sz.nz)), BF16),
            vm((nb, 3 * C[3] // nb, 128 * sz.nz), BF16),
            sems((2, 4, most)),
            sems((2, 4, most)),
            sems((2, nb)),
            sems((2, nb)),
            sems((2, nk)),
            sems((2, nk)),
        ]
    in_vmem = pl.BlockSpec(memory_space=pltpu.VMEM)
    in_smem = pl.BlockSpec(memory_space=pltpu.SMEM)
    got = pl.pallas_call(
        functools.partial(main_kernel, sz, nb, nk),
        out_shape=outs,
        in_specs=[in_smem] * 3
        + [in_vmem] * 5
        + [pl.BlockSpec(memory_space=pl.ANY)] * 4
        + [in_vmem] * (len(operands) - 12),
        out_specs=[in_vmem] * 5
        + [pl.BlockSpec(memory_space=pl.ANY)] * 2
        + [in_vmem],
        scratch_shapes=scratch,
        compiler_params=pltpu.CompilerParams(
            collective_id=0, has_side_effects=True, vmem_limit_bytes=60 * 2**20
        ),
    )(*operands)

    maps, sums, totals = got[0:5], got[5], got[-1]
    coarse = got[6]
    if not sz.gather:
        coarse = coarse.astype(BF16).reshape(2, 3, C[3], 3 * C[3])
        coarse = lax.psum(coarse, "rows")
        coarse = lax.psum_scatter(coarse, "batch", scatter_dimension=2, tiled=True)
        coarse = coarse.astype(F32).reshape(2, 3 * C[3] // nb, 3 * C[3])
    in_any = pl.BlockSpec(memory_space=pl.ANY)
    outs = [shape(m, BF16) for m in map_shapes]
    outs += [shape((2, 3, 3, C[l] // nb, C[l]), F32) for l in range(4)]
    outs += [shape((sz.uchan // nb, C[l]), F32) for l in range(1, 4)]
    outs += [shape((2, sz.total), F32)] * 2 + [shape((3, sz.uchan), F32)] * 2
    outs = pl.pallas_call(
        functools.partial(last_kernel, sz, nb),
        out_shape=outs,
        in_specs=[in_vmem] * 8,
        out_specs=[in_any] * 5 + [in_vmem] * (len(outs) - 5),
        scratch_shapes=[pltpu.SemaphoreType.DMA((5,))],
        compiler_params=pltpu.CompilerParams(vmem_limit_bytes=60 * 2**20),
    )(*maps, sums.reshape(2, sz.sum_rows, 128), totals, coarse)
    shaped = []
    for i, m in enumerate(outs[0:5]):
        l = max(i - 1, 0)
        if W[l] >= 128:
            shaped.append(m.reshape(1, C[l], R[l], W[l]))
        else:
            shaped.append(m.reshape(1, R[l], W[l], C[l]).transpose(0, 3, 1, 2))
    return (*shaped, *outs[5:])


def solution(mesh):
    image = P("batch", None, "rows", None)
    kernel = P(None, None, None, "batch", None)
    return jax.shard_map(
        body,
        mesh=mesh,
        in_specs=(image,) * 4 + (P(),) * 11 + (image,) + (P(),) * 3,
        out_specs=(image,) * 5 + (kernel,) * 4 + (P("batch", None),) * 3 + (P(),) * 4,
        check_vma=False,
    )
```

profile of v0, /device:TPU:0, one launch (start us, length us, event | category | flops | bytes accessed | tf_op | source)
XLA Modules:
  0.0 162.5 jit_solution(3530205638931653347)
XLA Ops:
  0.7 154.9 %shard_map.360 = (bf16[768,256]{1,0:T(8,128)(2,1)}, bf16[768,256]{1,0:T(8,128)(2,1)}, bf16[768,128]{1,0:T(8,128)(2,1)}, bf16[256,192]{1,0:T(8,128)(2,1)}, bf16[6...) custom-call(s32[4]{0:T(128)} %refs_0_.1, s32[4]{0:T(128)} %refs_1_.1, ...), custom_call_target="tpu_custom_call" | custom-call | tf_op jit(solution)/shard_map/pallas_call | solution.py:1465
  155.6 5.3 %shard_map.361 = (bf16[768,256]{1,0:T(8,128)(2,1)}, bf16[768,256]{1,0:T(8,128)(2,1)}, bf16[768,128]{1,0:T(8,128)(2,1)}, bf16[256,192]{1,0:T(8,128)(2,1)}, bf16[6...) custom-call(bf16[768,256]{1,0:T(8,128)(2,1)} %get-tuple-element.40.r, ...), custom_call_target="tpu_custom_call" | custom-call | tf_op jit(solution)/shard_map/pallas_call | solution.py:1493
  160.9 1.6 copy.41
where the time goes:
time: 163 us
  Pallas kernels  160 us (98%)
    pallas_call x1, Pallas kernels, body(): pl.pallas_call(functools.partial(main_kernel, sz, nb, nk), out_shape=outs...  155 us
    pallas_call x1, Pallas kernels, body(): pl.pallas_call(functools.partial(last_kernel, sz, nb), out_shape=outs, in...  5.3 us

commit v1 on v0

--- a/solution.py
+++ b/solution.py
@@ -45,20 +45,27 @@
         self.ny = nb // self.nc
         self.nz = nk // self.nx
         self.gather = nb * nk <= 32 and self.nx == 2 and self.nc == 2 and self.own[3] == 64
-        self.sum_levels = [0, 1, 2]
+        self.pair = self.gather and self.chan[2] // nb % 16 == 0 and self.own[2] % 128 == 0
+        self.sum_levels = [0, 1] if self.pair else [0, 1, 2]
         self.stacked = [l for l in range(3 if self.gather else 4) if self.width[l] < 128]
+        self.stacked = [l for l in self.stacked if not (self.pair and l == 2)]
         self.spots = {}
         at = 0
+
+        def place(key, values, width):
+            nonlocal at
+            rows = -(-values // 16) * 16
+            for i in range(-(-width // 128)):
+                self.spots[(*key, i)] = (at, rows)
+                at += rows
+
         for l in self.sum_levels:
-            rows = -(-3 * self.chan[l] // nb // 16) * 16
-            for i in range(-(-3 * self.chan[l] // 128)):
-                self.spots[l, i] = (at, rows)
-                at += rows
+            place((l,), 3 * self.chan[l] // nb, 3 * self.chan[l])
         for j in range(3):
-            rows = -(-self.uchan // nb // 16) * 16
-            for i in range(-(-self.chan[j + 1] // 128)):
-                self.spots["u", j, i] = (at, rows)
-                at += rows
+            place(("u", j), self.uchan // nb, self.chan[j + 1])
+        self.batch_rows = at
+        if self.pair:
+            place((2,), 3 * self.chan[2] // nb, 3 * self.chan[2])
         self.part = -(-at // (nk * 16)) * 16
         self.sum_rows = self.part * nk
 
@@ -131,11 +138,15 @@
     (sa_send, sa_recv, sb_send, sb_recv, rim_send, rim_recv) = take(6)
     raw_sem, wide_sem = take(2)
     prow, urow = take(2)
-    part_a, got_a, got_b, got_c, got_d, out_sem = take(6)
-    (ra_send, ra_recv, rb_send, rb_recv, rc_send, rc_recv, rd_send, rd_recv) = take(8)
+    part_a, got_a, got_b, part_s, got_x, got_z, got_d, out_sem = take(8)
+    (ra_send, ra_recv, rb_send, rb_recv, rx_send, rx_recv, rz_send, rz_recv) = take(8)
+    (dz_send, dz_recv, dx_send, dx_recv) = take(4)
     if sz.gather:
         xg, gs, gr, x3g, t3g = take(5)
-        (xg_send, xg_recv, g1_send, g1_recv, g2_send, g2_recv) = take(6)
+        (xg_send, xg_recv, g1_send, g1_recv, g2_send, g2_recv, g3_send, g3_recv) = take(8)
+    if sz.pair:
+        xb, x3b, gsb, gb, t3b = take(5)
+        (xb_send, xb_recv, gb_send, gb_recv) = take(4)
 
     C, R, W, N, NP, OFF = sz.chan, sz.rows, sz.width, sz.own, sz.flat, sz.off
     me_b = lax.axis_index("batch")
@@ -202,7 +213,6 @@
         pl.semaphore_signal(barrier, inc=1, device_id=(peer_b(j), me_k), device_id_type=MESH)
     for j in range(1, nk):
         pl.semaphore_signal(barrier, inc=1, device_id=(me_b, peer_k(j)), device_id_type=MESH)
-    pl.semaphore_wait(barrier, nb + nk - 2)
 
     my_h = jnp.int32(0)
     my_w = jnp.int32(0)
@@ -282,14 +292,19 @@
     def ucol(slot, j, lanes):
         return tile(ucols[slot, j * sz.uchan : (j + 1) * sz.uchan, :], lanes)
 
-    def to_columns(packed, ref, slot_list, blocks):
+    def to_columns(packed, ref, slot_list, spans):
         full = jnp.concatenate(packed + [jnp.zeros((128 - 8 * len(packed), 128), F32)], axis=0)
-        turned = full.T
+        standing = full.T
         for i, slot in enumerate(slot_list):
-            for k in range(blocks):
-                ref[slot, 128 * k : 128 * k + 128, :] = jnp.broadcast_to(
-                    turned[:, 8 * i + k : 8 * i + k + 1], (128, 128)
-                )
+            for lo, hi in spans:
+                for k in range(lo // 128, -(-hi // 128)):
+                    a, b = max(lo, 128 * k), min(hi, 128 * k + 128)
+                    v = standing[a - 128 * k : b - 128 * k, 8 * i + k : 8 * i + k + 1]
+                    ref[slot, a:b, :] = jnp.broadcast_to(v, (b - a, 128))
+
+    FINE, COARSE = (0,), (1, 2, 3)
+    spans_of = {FINE: [(0, C[0])], COARSE: [(C[0], sz.total)]}
+    u_spans = [(0, sz.utotal)]
 
     prow[...] = jnp.zeros_like(prow)
     urow[...] = jnp.zeros_like(urow)
@@ -326,84 +341,88 @@
 
     lane128 = lax.broadcasted_iota(jnp.int32, (1, 128), 1)
 
-    def record(a_ref, b_ref, blocks):
+    def record(a_ref, b_ref, spans):
         out = jnp.zeros((128, 128), F32)
         for base, ref in ((0, a_ref), (8, b_ref)):
-            for k in range(blocks):
-                s = jnp.sum(ref[128 * k : 128 * k + 128, :], axis=1, keepdims=True)
-                out = jnp.where(lane128 == base + k, s, out)
+            for lo, hi in spans:
+                for k in range(lo // 128, -(-hi // 128)):
+                    s = jnp.sum(ref[128 * k : 128 * k + 128, :], axis=1, keepdims=True)
+                    out = jnp.where(lane128 == base + k, s, out)
         return out.T[0:16]
 
-    def spread(e, which, rec, meanwhile):
-        copies = []
+    def record_copies(e, which, sending):
         if which == 0:
             ref, send, recv, n, me = rec_a, sa_send, sa_recv, nb, me_b
         else:
             ref, send, recv, n, me = rec_b, sb_send, sb_recv, nk, me_k
-        ref[e, me] = rec
+        out = []
         for j in range(1, n):
-            target = (peer_b(j), me_k) if which == 0 else (me_b, peer_k(j))
-            copy = pltpu.make_async_remote_copy(
-                src_ref=ref.at[e, me],
-                dst_ref=ref.at[e, me],
-                send_sem=send.at[e, j],
-                recv_sem=recv.at[e, me],
-                device_id=target,
-                device_id_type=MESH,
+            other = lax.rem(me + j, n)
+            slot = me if sending else other
+            out.append(
+                pltpu.make_async_remote_copy(
+                    src_ref=ref.at[e, me],
+                    dst_ref=ref.at[e, slot],
+                    send_sem=send.at[e, other],
+                    recv_sem=recv.at[e, slot],
+                    device_id=(other, me_k) if which == 0 else (me_b, other),
+                    device_id_type=MESH,
+                )
             )
+        return out
+
+    def record_send(e, which, rec):
+        if which == 0:
+            rec_a[e, me_b] = rec
+        else:
+            rec_b[e, me_k] = rec
+        for copy in record_copies(e, which, True):
             copy.start()
-            copies.append(copy)
-        if meanwhile is not None:
-            meanwhile()
-        for j in range(1, n):
-            other = peer_b(j) if which == 0 else peer_k(j)
-            pltpu.make_async_remote_copy(
-                src_ref=ref.at[e, me],
-                dst_ref=ref.at[e, other],
-                send_sem=send.at[e, j],
-                recv_sem=recv.at[e, other],
-                device_id=(me_b, me_k),
-                device_id_type=MESH,
-            ).wait_recv()
-        for copy in copies:
+
+    def record_total(e, which, sizes):
+        for copy in record_copies(e, which, False):
+            copy.wait_recv()
+        for copy in record_copies(e, which, True):
             copy.wait_send()
-
-    def gather_moments(e, rec, na_ref, nb_ref, meanwhile=(None, None)):
-        for which, n, ref, n_ref in ((0, nb, rec_a, na_ref), (1, nk, rec_b, nb_ref)):
-            spread(e, which, rec, meanwhile[which])
-            total = jnp.zeros((8, 128), F32)
-            size = jnp.zeros((8, 128), F32)
-            for i in range(n):
-                total = total + ref[e, i, 0:8]
-                size = size + n_ref[i]
-            mean = total / jnp.maximum(size, 1.0)
-            spread_sum = jnp.zeros((8, 128), F32)
-            for i in range(n):
-                delta = ref[e, i, 0:8] / jnp.maximum(n_ref[i], 1.0) - mean
-                spread_sum = spread_sum + (ref[e, i, 8:16] + n_ref[i] * delta * delta)
-            rec = jnp.concatenate([total, spread_sum], axis=0)
-        return rec
-
-    def gather_sums(e, rec, meanwhile=(None, None)):
-        for which, n, ref in ((0, nb, rec_a), (1, nk, rec_b)):
-            spread(e, which, rec, meanwhile[which])
-            rec = jnp.zeros((16, 128), F32)
-            for i in range(n):
-                rec = rec + ref[e, i]
-        return rec
+        ref, n = ((rec_a, nb), (rec_b, nk))[which]
+        if sizes is None:
+            out = ref[e, 0]
+            for i in range(1, n):
+                out = out + ref[e, i]
+            return out
+        total = jnp.zeros((8, 128), F32)
+        size = jnp.zeros((8, 128), F32)
+        for i in range(n):
+            total = total + ref[e, i, 0:8]
+            size = size + sizes[which][i]
+        mean = total / jnp.maximum(size, 1.0)
+        spread_sum = jnp.zeros((8, 128), F32)
+        for i in range(n):
+            delta = ref[e, i, 0:8] / jnp.maximum(sizes[which][i], 1.0) - mean
+            spread_sum = spread_sum + (ref[e, i, 8:16] + sizes[which][i] * delta * delta)
+        return jnp.concatenate([total, spread_sum], axis=0)
+
+    def ex_start(e, rec):
+        record_send(e, 0, rec)
+
+    def ex_mid(e, sizes=None):
+        record_send(e, 1, record_total(e, 0, sizes))
+
+    def ex_end(e, sizes=None):
+        return record_total(e, 1, sizes)
 
     def rim_copies(slot, src, dst):
         up = pltpu.make_async_remote_copy(
-            src_ref=src.at[0],
-            dst_ref=dst.at[1],
+            src_ref=src(0),
+            dst_ref=dst(1),
             send_sem=rim_send.at[slot, 0],
             recv_sem=rim_recv.at[slot, 1],
             device_id=(me_b, lax.rem(me_k + nk - 1, nk)),
             device_id_type=MESH,
         )
         down = pltpu.make_async_remote_copy(
-            src_ref=src.at[1],
-            dst_ref=dst.at[0],
+            src_ref=src(1),
+            dst_ref=dst(0),
             send_sem=rim_send.at[slot, 1],
             recv_sem=rim_recv.at[slot, 0],
             device_id=(me_b, lax.rem(me_k + 1, nk)),
@@ -466,15 +485,26 @@
             old = ref[g * rows : (g + 1) * rows, base : base + 128]
             ref[g * rows : (g + 1) * rows, base : base + 128] = jnp.where(here, v, old)
 
-    def pack_rims(slot, arrays):
-        for l in range(LEVELS):
-            at = slice(sz.rim_off[l], sz.rim_off[l] + sz.rim_rows[l])
+    def rim_span(group):
+        first, last = group[0], group[-1]
+        return slice(sz.rim_off[first], sz.rim_off[last] + sz.rim_rows[last])
+
+    def rims_of(slot, group):
+        at = rim_span(group)
+        number = 2 * slot + (0 if group == FINE else 1)
+        return number, lambda i: rim_s.at[i, at, :], lambda i: rim_r.at[slot, i, at, :]
+
+    def send_rims(slot, group, arrays):
+        for l in group:
+            at = rim_span((l,))
             rim_s[0, at, :] = pack_row(arrays[l], l, W[l]).astype(BF16)
             rim_s[1, at, :] = pack_row(arrays[l], l, N[l]).astype(BF16)
-
-    def unpack_rims(slot, arrays):
-        for l in range(LEVELS):
-            at = slice(sz.rim_off[l], sz.rim_off[l] + sz.rim_rows[l])
+        rims_start(*rims_of(slot, group))
+
+    def take_rims(slot, group, arrays):
+        rims_wait(*rims_of(slot, group))
+        for l in group:
+            at = rim_span((l,))
             unpack_row(arrays[l], l, 0, rim_r[slot, 0, at, :].astype(F32))
             unpack_row(arrays[l], l, W[l] + N[l], rim_r[slot, 1, at, :].astype(F32))
 
@@ -613,27 +643,42 @@
             out.append(remote(src, dst, rb_send.at[c, other], sem, target))
         return out
 
-    def row_copies(c, sending):
+    def part_at(x, z, n=1):
+        return pl.ds(pl.multiple_of((x * nz + z) * sz.part, 16), n * sz.part)
+
+    def x_copies(c):
         out = []
-        for other in others(nk, me_k):
-            slot = me_k if sending else other
-            out.append(
-                remote(
-                    part_a.at[c, my_core, my_y, pl.ds(pl.multiple_of(other * sz.part, 16), sz.part), :],
-                    got_c.at[c, slot], rc_send.at[c, other], rc_recv.at[c, slot], (me_b, other)
-                )
-            )
+        for other in others(nx, my_x):
+            src = part_s.at[c, part_at(other, 0, nz), :]
+            target = (me_b, my_z * nx + other)
+            out.append(remote(src, got_x.at[c], rx_send.at[c], rx_recv.at[c], target))
         return out
 
-    def back_copies(c, sending):
+    def z_copies(c, sending):
         out = []
-        for other in others(nk, me_k):
-            slot = me_k if sending else other
-            out.append(
-                remote(
-                    got_d.at[c, me_k], got_d.at[c, slot], rd_send.at[c, other], rd_recv.at[c, slot], (me_b, other)
-                )
-            )
+        for other in others(nz, my_z):
+            slot = my_z if sending else other
+            src = part_s.at[c, part_at(my_x, other), :]
+            target = (me_b, other * nx + my_x)
+            out.append(remote(src, got_z.at[c, slot], rz_send.at[c, other], rz_recv.at[c, slot], target))
+        return out
+
+    def back_z_copies(c, sending):
+        out = []
+        for other in others(nz, my_z):
+            slot = my_z if sending else other
+            src, dst = got_d.at[c, part_at(my_x, my_z), :], got_d.at[c, part_at(my_x, slot), :]
+            target = (me_b, other * nx + my_x)
+            out.append(remote(src, dst, dz_send.at[c, other], dz_recv.at[c, slot], target))
+        return out
+
+    def back_x_copies(c, sending):
+        out = []
+        for other in others(nx, my_x):
+            slot = my_x if sending else other
+            src, dst = got_d.at[c, part_at(my_x, 0, nz), :], got_d.at[c, part_at(slot, 0, nz), :]
+            target = (me_b, my_z * nx + other)
+            out.append(remote(src, dst, dx_send.at[c], dx_recv.at[c], target))
         return out
 
     def finish(pair):
@@ -643,12 +688,11 @@
         for copy in sent:
             copy.wait_send()
 
-    def sum_first(c, src):
-        for l in sz.sum_levels:
-            kernel_grad(l, src)
-            sum_pack(c, l)
-        if c == 1:
-            sum_pack_unites()
+    def sum_level(c, l, src):
+        kernel_grad(l, src)
+        sum_pack(c, l)
+
+    def sum_first(c):
         for copy in core_copies(c):
             copy.start()
 
@@ -666,29 +710,129 @@
     def sum_third(c):
         finish((y_copies(c, True), y_copies(c, False)))
         got_b[c, my_y] = part_a[c, my_core, my_y]
-        for k in range(nk):
-            at = slice(k * sz.part, (k + 1) * sz.part)
-            v = got_b[c, 0, at, :].astype(F32)
-            for y in range(1, ny):
-                v = v + got_b[c, y, at, :].astype(F32)
-            part_a[c, my_core, my_y, at, :] = v.astype(BF16)
-        for copy in row_copies(c, True):
+        v = got_b[c, 0].astype(F32)
+        for y in range(1, ny):
+            v = v + got_b[c, y].astype(F32)
+        part_s[c, 0 : sz.batch_rows, :] = v.astype(BF16)
+        for copy in x_copies(c):
             copy.start()
 
     def sum_fourth(c):
-        finish((row_copies(c, True), row_copies(c, False)))
-        mine = pl.ds(pl.multiple_of(me_k * sz.part, 16), sz.part)
-        got_c[c, me_k] = part_a[c, my_core, my_y, mine, :]
-        v = got_c[c, 0].astype(F32)
-        for k in range(1, nk):
-            v = v + got_c[c, k].astype(F32)
-        got_d[c, me_k] = v.astype(BF16)
-        for copy in back_copies(c, True):
+        copies = x_copies(c)
+        finish((copies, copies))
+        mine = part_at(my_x, 0, nz)
+        if nx > 1:
+            v = part_s[c, mine, :].astype(F32) + got_x[c].astype(F32)
+            part_s[c, mine, :] = v.astype(BF16)
+        for copy in z_copies(c, True):
             copy.start()
 
+    def sum_fifth(c):
+        finish((z_copies(c, True), z_copies(c, False)))
+        got_z[c, my_z] = part_s[c, part_at(my_x, my_z), :]
+        v = got_z[c, 0].astype(F32)
+        for z in range(1, nz):
+            v = v + got_z[c, z].astype(F32)
+        got_d[c, part_at(my_x, my_z), :] = v.astype(BF16)
+        for copy in back_z_copies(c, True):
+            copy.start()
+
+    def sum_sixth(c):
+        finish((back_z_copies(c, True), back_z_copies(c, False)))
+        for copy in back_x_copies(c, True):
+            copy.start()
+
     def sum_last(c):
-        finish((back_copies(c, True), back_copies(c, False)))
+        finish((back_x_copies(c, True), back_x_copies(c, False)))
         pltpu.make_async_copy(got_d.at[c], sums_ref.at[c], out_sem.at[c]).start()
+
+    c2 = C[2] // nb
+
+    def pair_copies(c, step, sending):
+        if not sz.pair:
+            return []
+        n, me = ((ny, my_y), (nc, my_core))[step]
+        out = []
+        for other in others(n, me):
+            slot = me if sending else other
+            if step == 0:
+                ref, target = xb.at[c, my_core, slot], (other * nc + my_core, me_k)
+            else:
+                ref, target = xb.at[c, slot], (my_y * nc + other, me_k)
+            out.append(remote(ref, ref, xb_send.at[c, step, other], xb_recv.at[c, step, slot], target))
+        return out
+
+    def pair_begin(c, ref):
+        if sz.pair:
+            xb[c, my_core, my_y] = ref[2][C[2] : 2 * C[2], :]
+            for copy in pair_copies(c, 0, True):
+                copy.start()
+
+    def pair_next(c):
+        finish((pair_copies(c, 0, True), pair_copies(c, 0, False)))
+        for copy in pair_copies(c, 1, True):
+            copy.start()
+
+    def pair_inputs(c):
+        if not sz.pair:
+            return
+        finish((pair_copies(c, 1, True), pair_copies(c, 1, False)))
+        at = lax.broadcasted_iota(jnp.int32, (1, NP[2]), 1) & (W[2] - 1)
+
+        def item(b, _):
+            def group(q, _):
+                rows = pl.ds(pl.multiple_of(q * c2, 16), c2)
+                v = xb[c, lax.rem(b, nc), lax.div(b, nc), rows, :].astype(F32)
+                left = jnp.where(at == 0, 0.0, pltpu.roll(v, 1, 1))
+                right = jnp.where(at == W[2] - 1, 0.0, pltpu.roll(v, NP[2] - 1, 1))
+                for u, part in enumerate((left, v, right)):
+                    x3b[b, pl.ds(pl.multiple_of(u * C[2] + q * c2, 16), c2), :] = part.astype(BF16)
+                return 0
+
+            lax.fori_loop(0, nb, group, 0)
+            return 0
+
+        lax.fori_loop(0, nb, item, 0)
+
+    def pair_grad_copies(c, sending):
+        out = []
+        for other in others(nb, me_b):
+            slot = me_b if sending else other
+            out.append(
+                remote(gsb.at[c, other], gb.at[c, slot], gb_send.at[c, other], gb_recv.at[c, slot], (other, me_k))
+            )
+        return out
+
+    def pair_grad_begin(c):
+        if sz.pair:
+            for q in range(nb):
+                v = g3[2][C[2] + q * c2 : C[2] + (q + 1) * c2, :].astype(F32)
+                gsb[c, q] = pltpu.roll(v, NP[2] - W[2], 1)[:, 0 : N[2]].astype(BF16)
+            for copy in pair_grad_copies(c, True):
+                copy.start()
+
+    def pair_gradient(c):
+        if not sz.pair:
+            return
+        finish((pair_grad_copies(c, True), pair_grad_copies(c, False)))
+        gb[c, me_b] = gsb[c, me_b]
+
+        def item(b, _):
+            v = jnp.concatenate([gb[c, b].astype(F32), jnp.zeros((c2, NP[2] - N[2]), F32)], axis=1)
+            for t in range(3):
+                part = pltpu.roll(v, t * W[2], 1) if t else v
+                t3b[b, t * c2 : (t + 1) * c2, :] = part.astype(BF16)
+            return 0
+
+        lax.fori_loop(0, nb, item, 0)
+        acc = None
+        for b in range(nb):
+            part = lax.dot_general(t3b[b], x3b[b], (((1,), (1,)), ((), ())), preferred_element_type=F32)
+            acc = part if acc is None else acc + part
+        for i in range(-(-3 * C[2] // 128)):
+            at, rows = sz.spots[2, i]
+            m = min(128, 3 * C[2] - 128 * i)
+            part_s[c, at : at + rows, 0:m] = acc[:, 128 * i : 128 * i + m].astype(BF16)
 
     c3 = C[3] // nb
     half = c3 // 2
@@ -749,13 +893,20 @@
                 slot = me_b if sending else other
                 src = gs.at[c, other]
                 out.append(
-                    remote(src, gr.at[c, me_k, slot], g1_send.at[c, other], g1_recv.at[c, slot], (other, me_k))
+                    remote(src, gr.at[c, my_x, my_z, slot], g1_send.at[c, other], g1_recv.at[c, slot], (other, me_k))
                 )
+        elif step == 1:
+            for other in others(nz, my_z):
+                slot = my_z if sending else other
+                src, dst = gr.at[c, my_x, my_z], gr.at[c, my_x, slot]
+                target = (me_b, other * nx + my_x)
+                out.append(remote(src, dst, g2_send.at[c, other], g2_recv.at[c, slot], target))
         else:
-            for other in others(nk, me_k):
-                slot = me_k if sending else other
-                ref = gr.at[c, slot]
-                out.append(remote(gr.at[c, me_k], ref, g2_send.at[c, other], g2_recv.at[c, slot], (me_b, other)))
+            for other in others(nx, my_x):
+                slot = my_x if sending else other
+                src, dst = gr.at[c, my_x], gr.at[c, slot]
+                target = (me_b, my_z * nx + other)
+                out.append(remote(src, dst, g3_send.at[c], g3_recv.at[c], target))
         return out
 
     def grad_begin(c):
@@ -769,8 +920,14 @@
     def grad_next(c):
         if sz.gather:
             finish((grad_copies(c, 0, True), grad_copies(c, 0, False)))
-            gr[c, me_k, me_b] = gs[c, me_b]
+            gr[c, my_x, my_z, me_b] = gs[c, me_b]
             for copy in grad_copies(c, 1, True):
+                copy.start()
+
+    def grad_third(c):
+        if sz.gather:
+            finish((grad_copies(c, 1, True), grad_copies(c, 1, False)))
+            for copy in grad_copies(c, 2, True):
                 copy.start()
 
     image = nz * 128
@@ -822,13 +979,13 @@
         if not sz.gather:
             coarse_local(c, a3 if c else x3)
             return
-        finish((grad_copies(c, 1, True), grad_copies(c, 1, False)))
+        finish((grad_copies(c, 2, True), grad_copies(c, 2, False)))
         lane = lax.broadcasted_iota(jnp.int32, (1, image), 1)
 
         def item(b, _):
             low, high = [], []
             for z in range(nz):
-                first, second = unpack_pixels(gr[c, nx * z, b], gr[c, nx * z + 1, b])
+                first, second = unpack_pixels(gr[c, 0, z, b], gr[c, 1, z, b])
                 low.append(first)
                 high.append(second)
             for i, parts in enumerate((low, high)):
@@ -864,8 +1021,8 @@
         coarse_copy(c, 1).wait()
         coarse_copy(c, 2).wait()
 
-    def moments(arrays):
-        for l in range(LEVELS):
+    def moments(arrays, group):
+        for l in group:
 
             def body(r0, rc, lanes, l=l):
                 acc = jnp.zeros((rc, 128), F32)
@@ -875,11 +1032,11 @@
                 stat_a[pl.ds(pl.multiple_of(OFF[l] + r0, 16), rc), :] = acc
 
             each(l, body)
-        for l in range(LEVELS):
+        for l in group:
             at = slice(OFF[l], OFF[l] + C[l])
             s = jnp.sum(stat_a[at, :], axis=1, keepdims=True) * inv_local[l]
             cols[LOCAL, at, :] = jnp.broadcast_to(s, (C[l], 128))
-        for l in range(LEVELS):
+        for l in group:
 
             def body(r0, rc, lanes, l=l):
                 acc = jnp.zeros((rc, 128), F32)
@@ -891,7 +1048,12 @@
                 stat_b[pl.ds(pl.multiple_of(OFF[l] + r0, 16), rc), :] = acc
 
             each(l, body)
-        return record(stat_a, stat_b, sz.blocks)
+        return record(stat_a, stat_b, spans_of[group])
+
+    def mean_rstd(got, group):
+        mean, rstd = got[0:8] * inv_count, lax.rsqrt(got[8:16] * inv_count + EPSILON)
+        to_columns([mean, rstd], cols, [MEAN, RSTD], spans_of[group])
+        return rstd
 
     def halves(l):
         return max(1, W[l] // 128)
@@ -911,44 +1073,25 @@
             v = feats[l][...].astype(F32)
             v = jnp.concatenate([v, jnp.zeros((NP[l] - N[l], C[l]), F32)], axis=0)
             xf[l][...] = pltpu.roll(v.T, W[l], 1)
-    pack_rims(0, xf)
-    rims_start(0, rim_s, rim_r.at[0])
+    pl.semaphore_wait(barrier, nb + nk - 2)
+    send_rims(0, COARSE, xf)
+    send_rims(0, FINE, xf)
     to_stage(stage, ograd)
     widen(0)
-    rims_wait(0, rim_s, rim_r.at[0])
-    unpack_rims(0, xf)
-    for l in range(LEVELS):
-
-        def body(r0, rc, lanes, l=l):
+
+    def stack_start(l):
+        def body(r0, rc, lanes):
             for a, b in lane_chunks(l, lanes):
                 m = masks[l][0:1, a:b] > 0
                 stack_columns(x3[l], l, r0, rc, a, b, jnp.where(m, xf[l][pl.ds(r0, rc), a:b], 0.0))
 
         each(l, body)
 
-    gather_begin(0, x3)
-    for l in range(LEVELS):
-        conv(l, wide, 0, x3, y1)
-    pack_rims(1, y1)
-    rims_start(1, rim_s, rim_r.at[1])
-
-    def while_first():
-        gather_next(0, 0)
-        turn(0)
-
-    got = gather_moments(0, moments(y1), n_a, n_b, (while_first, lambda: widen(1)))
-    rims_wait(1, rim_s, rim_r.at[1])
-    mean1_p = got[0:8] * inv_count
-    rstd1_p = lax.rsqrt(got[8:16] * inv_count + EPSILON)
-    to_columns([mean1_p, rstd1_p], cols, [MEAN, RSTD], sz.blocks)
-    unpack_rims(1, y1)
-
     def pre_of(hat, gain, shift, l, r0, rc, lanes):
         return hat * col(gain, l, r0, rc, lanes) + col(shift, l, r0, rc, lanes)
 
-    for l in range(LEVELS):
-
-        def body(r0, rc, lanes, l=l):
+    def first_act(l):
+        def body(r0, rc, lanes):
             for a, b in lane_chunks(l, lanes):
                 m = masks[l][0:1, a:b] > 0
                 hat = (y1[l][pl.ds(r0, rc), a:b] - col(MEAN, l, r0, rc, lanes)) * col(RSTD, l, r0, rc, lanes)
@@ -958,40 +1101,147 @@
 
         each(l, body)
 
-    gather_begin(1, a3)
-    for l in range(LEVELS):
-        conv(l, wide, 1, a3, y2)
-    pack_rims(2, y2)
-    rims_start(2, rim_s, rim_r.at[2])
-
-    def while_second():
-        gather_next(0, 1)
-        gather_next(1, 0)
-
-    got = gather_moments(1, moments(y2), n_a, n_b, (while_second, lambda: turn(1)))
-    rims_wait(2, rim_s, rim_r.at[2])
-    mean2_p = got[0:8] * inv_count
-    rstd2_p = lax.rsqrt(got[8:16] * inv_count + EPSILON)
-    to_columns([mean2_p, rstd2_p], cols, [MEAN, RSTD], sz.blocks)
-    unpack_rims(2, y2)
-
-    def start_part(l, r0, rc, a, b):
-        return x3[l][pl.ds(pl.multiple_of(C[l] + r0, 16), rc), a:b].astype(F32)
-
-    for l in range(LEVELS):
-
-        def body(r0, rc, lanes, l=l):
+    def second_act(l):
+        def body(r0, rc, lanes):
             for a, b in lane_chunks(l, lanes):
                 m = masks[l][0:1, a:b] > 0
                 hat = (y2[l][pl.ds(r0, rc), a:b] - col(MEAN, l, r0, rc, lanes)) * col(RSTD, l, r0, rc, lanes)
                 y2[l][pl.ds(r0, rc), a:b] = hat
                 pre = pre_of(hat, GAIN2, SHIFT2, l, r0, rc, lanes)
-                pre = jnp.where(m, pre, 0.0) + start_part(l, r0, rc, a, b)
+                start = x3[l][pl.ds(pl.multiple_of(C[l] + r0, 16), rc), a:b].astype(F32)
+                pre = jnp.where(m, pre, 0.0) + start
                 p1[l][pl.ds(r0, rc), a:b] = pre
                 if l:
                     br[l - 1][pl.ds(r0, rc), a:b] = (pre * sigmoid(pre)).astype(BF16)
 
         each(l, body)
+
+    def second_sums(l):
+        def body(r0, rc, lanes):
+            acc_g = jnp.zeros((rc, 128), F32)
+            acc_s = jnp.zeros((rc, 128), F32)
+            for a, b in lane_chunks(l, lanes):
+                m = masks[l][1:2, a:b] > 0
+                pre = p1[l][pl.ds(r0, rc), a:b]
+                sig = sigmoid(pre)
+                d = xf[l][pl.ds(r0, rc), a:b] * (sig * (1.0 + pre * (1.0 - sig)))
+                xf[l][pl.ds(r0, rc), a:b] = d
+                d = jnp.where(m, d, 0.0)
+                acc_s = acc_s + fold(d)
+                acc_g = acc_g + fold(jnp.where(m, d * y2[l][pl.ds(r0, rc), a:b], 0.0))
+            at = pl.ds(pl.multiple_of(OFF[l] + r0, 16), rc)
+            stat_a[at, :] = acc_g
+            stat_b[at, :] = acc_s
+
+        each(l, body)
+
+    def first_sums(l):
+        def body(r0, rc, lanes):
+            acc_g = jnp.zeros((rc, 128), F32)
+            acc_s = jnp.zeros((rc, 128), F32)
+            for a, b in lane_chunks(l, lanes):
+                m = masks[l][1:2, a:b] > 0
+                hat = y1[l][pl.ds(r0, rc), a:b]
+                pre = pre_of(hat, GAIN1, SHIFT1, l, r0, rc, lanes)
+                sig = sigmoid(pre)
+                d = p1[l][pl.ds(r0, rc), a:b] * (sig * (1.0 + pre * (1.0 - sig)))
+                d = jnp.where(m, d, 0.0)
+                p1[l][pl.ds(r0, rc), a:b] = d
+                acc_s = acc_s + fold(d)
+                acc_g = acc_g + fold(jnp.where(m, d * hat, 0.0))
+            at = pl.ds(pl.multiple_of(OFF[l] + r0, 16), rc)
+            stat_a[at, :] = acc_g
+            stat_b[at, :] = acc_s
+
+        each(l, body)
+
+    def norm_grad(l, hats, grads):
+        def body(r0, rc, lanes):
+            parts = []
+            for a, b in lane_chunks(l, lanes):
+                m = masks[l][0:1, a:b] > 0
+                hat = hats[l][pl.ds(r0, rc), a:b]
+                d = grads[l][pl.ds(r0, rc), a:b]
+                g = col(CA, l, r0, rc, lanes) * (
+                    d - col(CB, l, r0, rc, lanes) - hat * col(CC, l, r0, rc, lanes)
+                )
+                g = jnp.where(m, g, 0.0)
+                stack_columns(g3[l], l, r0, rc, a, b, g, back=True)
+                parts.append(g)
+            if l in sz.stacked:
+                v = parts[0] if len(parts) == 1 else jnp.concatenate(parts, axis=1)
+                stack_rows(t3[l], l, r0, rc, jnp.where(masks[l][1:2, :] > 0, v, 0.0))
+
+        each(l, body)
+
+    def norm_columns(scale, got, group):
+        to_columns(
+            [scale, got[8:16] * inv_count, got[0:8] * inv_count], cols, [CA, CB, CC], spans_of[group]
+        )
+
+    def features_out(l):
+        if W[l] < 128:
+            v = jnp.where(masks[l][1:2, :] > 0, y1[l][...] + xf[l][...], 0.0)
+            gfeat[l][...] = pltpu.roll(v, NP[l] - W[l], 1).T[0 : N[l]].astype(BF16)
+            return
+
+        def body(r0, rc, lanes):
+            for r in range(R[l]):
+                for h in range(halves(l)):
+                    a = (r + 1) * W[l] + 128 * h
+                    m = masks[l][1:2, a : a + 128] > 0
+                    v = y1[l][pl.ds(r0, rc), a : a + 128] + xf[l][pl.ds(r0, rc), a : a + 128]
+                    stage[h, pl.ds(r0 * R[l] + r, rc, stride=R[l]), :] = jnp.where(m, v, 0.0)
+
+        each(l, body)
+        for h in range(halves(l)):
+            gfeat[l][:, 128 * h : 128 * h + 128] = stage[h].astype(BF16)
+
+    sizes, u_sizes = (n_a, n_b), (un_a, un_b)
+    fine_place = place < C[0]
+
+    take_rims(0, COARSE, xf)
+    for l in COARSE:
+        stack_start(l)
+    gather_begin(0, x3)
+    for l in COARSE:
+        conv(l, wide, 0, x3, y1)
+    send_rims(1, COARSE, y1)
+    ex_start(0, moments(y1, COARSE))
+    take_rims(0, FINE, xf)
+    stack_start(0)
+    conv(0, wide, 0, x3, y1)
+    send_rims(1, FINE, y1)
+    ex_mid(0, sizes)
+    ex_start(1, moments(y1, FINE))
+    pair_begin(0, x3)
+    turn(0)
+    ex_mid(1, sizes)
+    gather_next(0, 0)
+    widen(1)
+    rstd1_c = mean_rstd(ex_end(0, sizes), COARSE)
+    take_rims(1, COARSE, y1)
+    for l in COARSE:
+        first_act(l)
+
+    gather_begin(1, a3)
+    for l in COARSE:
+        conv(l, wide, 1, a3, y2)
+    send_rims(2, COARSE, y2)
+    ex_start(2, moments(y2, COARSE))
+    rstd1_f = mean_rstd(ex_end(1, sizes), FINE)
+    take_rims(1, FINE, y1)
+    first_act(0)
+    ex_mid(2, sizes)
+    conv(0, wide, 1, a3, y2)
+    send_rims(2, FINE, y2)
+    ex_start(4, moments(y2, FINE))
+    pair_begin(1, a3)
+    pair_next(0)
+    rstd2_c = mean_rstd(ex_end(2, sizes), COARSE)
+    take_rims(2, COARSE, y2)
+    for l in COARSE:
+        second_act(l)
 
     UC_ = sz.uchan
     for j in range(3):
@@ -1006,15 +1256,20 @@
         mean = jnp.sum(part, axis=1, keepdims=True) * inv_local[l]
         d = jnp.where(m, uo[j][...] - mean, 0.0)
         ustat_b[j * UC_ : (j + 1) * UC_, :] = fold(d * d)
-
-    def while_unite():
-        gather_next(0, 2)
-        gather_next(1, 1)
-
-    got = gather_moments(2, record(ustat_a, ustat_b, sz.ublocks), un_a, un_b, (while_unite, None))
+    ex_start(3, record(ustat_a, ustat_b, u_spans))
+    ex_mid(4, sizes)
+    gather_next(0, 1)
+    turn(1)
+    ex_mid(3, u_sizes)
+    gather_next(1, 0)
+    pair_next(1)
+    rstd2_f = mean_rstd(ex_end(4, sizes), FINE)
+    take_rims(2, FINE, y2)
+    second_act(0)
+    got = ex_end(3, u_sizes)
     umean_p = got[0:8] * inv_ucount
     urstd_p = lax.rsqrt(got[8:16] * inv_ucount + EPSILON)
-    to_columns([umean_p, urstd_p], ucols, [UMEAN, URSTD], sz.ublocks)
+    to_columns([umean_p, urstd_p], ucols, [UMEAN, URSTD], u_spans)
 
     at_top = me_k == 0
     at_bottom = me_k == nk - 1
@@ -1022,8 +1277,7 @@
     split = lambda v: (v.astype(BF16), (v - v.astype(BF16).astype(F32)).astype(BF16))
 
     def edge(l, n):
-        lane = lax.broadcasted_iota(jnp.int32, (1, n), 1)
-        return lane
+        return lax.broadcasted_iota(jnp.int32, (1, n), 1)
 
     for j in range(3):
         l = j + 1
@@ -1084,7 +1338,6 @@
     for h in range(halves(0)):
         united_ref[:, 128 * h : 128 * h + 128] = stage[h].astype(BF16)
 
-    ud = []
     for j in range(3):
         l = j + 1
         span = max(128, W[l])
@@ -1117,16 +1370,23 @@
         at += n
     mid_s[0, :, at : at + fine] = xf[0][:, fine : 2 * fine].astype(BF16)
     mid_s[1, :, at : at + fine] = xf[0][:, N[0] : N[0] + fine].astype(BF16)
-    rims_start(3, mid_s, mid_r)
-    got4 = gather_sums(3, record(ustat_a, ustat_b, sz.ublocks), (lambda: gather_next(1, 2), None))
-    totals_ref[0] = got4
-    rims_wait(3, mid_s, mid_r)
-    scale_p = urstd_p * ugain_p
+    rims_start(8, lambda i: mid_s.at[i], lambda i: mid_r.at[i])
+    ex_start(5, record(ustat_a, ustat_b, u_spans))
+    second_sums(0)
+    ex_mid(5)
+    ex_start(6, record(stat_a, stat_b, spans_of[FINE]))
+    gather_next(1, 1)
+    got = ex_end(5)
+    totals_ref[0] = got
+    rims_wait(8, lambda i: mid_s.at[i], lambda i: mid_r.at[i])
     to_columns(
-        [scale_p, got4[8:16] * inv_ucount, got4[0:8] * inv_ucount], ucols, [UA, UB, UC], sz.ublocks
+        [urstd_p * ugain_p, got[8:16] * inv_ucount, got[0:8] * inv_ucount], ucols, [UA, UB, UC], u_spans
     )
-    xf[0][:, 0:fine] = mid_r[0, :, at : at + fine].astype(F32)
-    xf[0][:, N[0] + fine : NP[0]] = mid_r[1, :, at : at + fine].astype(F32)
+    for i, lane0 in ((0, 0), (1, W[0] + N[0])):
+        pre = p1[0][:, lane0 : lane0 + fine]
+        sig = sigmoid(pre)
+        slope = sig * (1.0 + pre * (1.0 - sig))
+        xf[0][:, lane0 : lane0 + fine] = mid_r[i, :, at : at + fine].astype(F32) * slope
     for j in range(3):
         l = j + 1
         start, n = lay[j]
@@ -1156,151 +1416,89 @@
             own, br[j][...], (((1,), (1,)), ((), ())), preferred_element_type=F32
         )
 
-    for l in range(LEVELS):
-
-        def body(r0, rc, lanes, l=l):
-            acc_g = jnp.zeros((rc, 128), F32)
-            acc_s = jnp.zeros((rc, 128), F32)
-            for a, b in lane_chunks(l, lanes):
-                m = masks[l][1:2, a:b] > 0
-                pre = p1[l][pl.ds(r0, rc), a:b]
-                sig = sigmoid(pre)
-                d = xf[l][pl.ds(r0, rc), a:b] * (sig * (1.0 + pre * (1.0 - sig)))
-                xf[l][pl.ds(r0, rc), a:b] = d
-                d = jnp.where(m, d, 0.0)
-                acc_s = acc_s + fold(d)
-                acc_g = acc_g + fold(jnp.where(m, d * y2[l][pl.ds(r0, rc), a:b], 0.0))
-            at = pl.ds(pl.multiple_of(OFF[l] + r0, 16), rc)
-            stat_a[at, :] = acc_g
-            stat_b[at, :] = acc_s
-
-        each(l, body)
-    got5 = gather_sums(4, record(stat_a, stat_b, sz.blocks), (lambda: coarse_inputs(1), None))
-    totals_ref[1] = got5
-    to_columns(
-        [rstd2_p * gain2_p, got5[8:16] * inv_count, got5[0:8] * inv_count], cols, [CA, CB, CC], sz.blocks
-    )
-
-    def store_gradient(l, r0, rc, parts):
-        v = parts[0] if len(parts) == 1 else jnp.concatenate(parts, axis=1)
-        if l not in sz.stacked:
-            return
-        stack_rows(t3[l], l, r0, rc, jnp.where(masks[l][1:2, :] > 0, v, 0.0))
-
-    for l in range(LEVELS):
-
-        def body(r0, rc, lanes, l=l):
-            parts = []
-            for a, b in lane_chunks(l, lanes):
-                m = masks[l][0:1, a:b] > 0
-                hat = y2[l][pl.ds(r0, rc), a:b]
-                d = xf[l][pl.ds(r0, rc), a:b]
-                g = col(CA, l, r0, rc, lanes) * (
-                    d - col(CB, l, r0, rc, lanes) - hat * col(CC, l, r0, rc, lanes)
-                )
-                g = jnp.where(m, g, 0.0)
-                stack_columns(g3[l], l, r0, rc, a, b, g, back=True)
-                parts.append(g)
-            store_gradient(l, r0, rc, parts)
-
-        each(l, body)
-
+    for l in COARSE:
+        second_sums(l)
+    ex_start(7, record(stat_a, stat_b, spans_of[COARSE]))
+    ex_mid(6)
+    got_f = ex_end(6)
+    norm_columns(rstd2_f * gain2_p, got_f, FINE)
+    norm_grad(0, y2, xf)
+    ex_mid(7)
+    conv(0, wide, 1, g3, p1, -1)
+    first_sums(0)
+    send_rims(3, FINE, p1)
+    ex_start(8, record(stat_a, stat_b, spans_of[FINE]))
+    sum_level(1, 0, a3)
+    sum_pack_unites()
+    got = ex_end(7)
+    totals_ref[1] = jnp.where(jnp.concatenate([fine_place] * 2, axis=0), got_f, got)
+    norm_columns(rstd2_c * gain2_p, got, COARSE)
+    norm_grad(2, y2, xf)
+    pair_grad_begin(1)
+    norm_grad(3, y2, xf)
     grad_begin(1)
-
-    for l in range(LEVELS):
+    norm_grad(1, y2, xf)
+
+    for l in COARSE:
         conv(l, wide, 1, g3, p1, -1)
-    for l in range(LEVELS):
-
-        def body(r0, rc, lanes, l=l):
-            acc_g = jnp.zeros((rc, 128), F32)
-            acc_s = jnp.zeros((rc, 128), F32)
-            for a, b in lane_chunks(l, lanes):
-                m = masks[l][1:2, a:b] > 0
-                hat = y1[l][pl.ds(r0, rc), a:b]
-                pre = pre_of(hat, GAIN1, SHIFT1, l, r0, rc, lanes)
-                sig = sigmoid(pre)
-                d = p1[l][pl.ds(r0, rc), a:b] * (sig * (1.0 + pre * (1.0 - sig)))
-                d = jnp.where(m, d, 0.0)
-                p1[l][pl.ds(r0, rc), a:b] = d
-                acc_s = acc_s + fold(d)
-                acc_g = acc_g + fold(jnp.where(m, d * hat, 0.0))
-            at = pl.ds(pl.multiple_of(OFF[l] + r0, 16), rc)
-            stat_a[at, :] = acc_g
-            stat_b[at, :] = acc_s
-
-        each(l, body)
-    pack_rims(3, p1)
-    rims_start(4, rim_s, rim_r.at[3])
-
-    def while_back():
-        grad_next(1)
-        sum_first(1, a3)
-
-    def while_back_rows():
-        coarse_gradient(1)
-        coarse_inputs(0)
-
-    got6 = gather_sums(5, record(stat_a, stat_b, sz.blocks), (while_back, while_back_rows))
-    totals_ref[2] = got6
-    rims_wait(4, rim_s, rim_r.at[3])
-    to_columns(
-        [rstd1_p * gain1_p, got6[8:16] * inv_count, got6[0:8] * inv_count], cols, [CA, CB, CC], sz.blocks
-    )
-    unpack_rims(3, p1)
-    for l in (3, 0, 1, 2):
-
-        def body(r0, rc, lanes, l=l):
-            parts = []
-            for a, b in lane_chunks(l, lanes):
-                m = masks[l][0:1, a:b] > 0
-                hat = y1[l][pl.ds(r0, rc), a:b]
-                d = p1[l][pl.ds(r0, rc), a:b]
-                g = col(CA, l, r0, rc, lanes) * (
-                    d - col(CB, l, r0, rc, lanes) - hat * col(CC, l, r0, rc, lanes)
-                )
-                g = jnp.where(m, g, 0.0)
-                stack_columns(g3[l], l, r0, rc, a, b, g, back=True)
-                parts.append(g)
-            store_gradient(l, r0, rc, parts)
-
-        each(l, body)
-        if l == 3:
-            grad_begin(0)
-
-    sum_first(0, x3)
+    for l in COARSE:
+        first_sums(l)
+    send_rims(3, COARSE, p1)
+    ex_start(9, record(stat_a, stat_b, spans_of[COARSE]))
+    for l in sz.sum_levels[1:]:
+        sum_level(1, l, a3)
+    sum_first(1)
+    ex_mid(8)
+    pair_inputs(1)
+    ex_mid(9)
     sum_second(1)
+    grad_next(1)
+    pair_gradient(1)
+    gather_next(0, 2)
+    gather_next(1, 2)
+    got_f = ex_end(8)
+    take_rims(3, FINE, p1)
+    norm_columns(rstd1_f * gain1_p, got_f, FINE)
+    norm_grad(0, y1, p1)
+    sum_third(1)
+    sum_level(0, 0, x3)
+    grad_third(1)
+    got = ex_end(9)
+    totals_ref[2] = jnp.where(jnp.concatenate([fine_place] * 2, axis=0), got_f, got)
+    take_rims(3, COARSE, p1)
+    norm_columns(rstd1_c * gain1_p, got, COARSE)
+    norm_grad(2, y1, p1)
+    pair_grad_begin(0)
+    norm_grad(3, y1, p1)
+    grad_begin(0)
+    norm_grad(1, y1, p1)
+    for l in sz.sum_levels[1:]:
+        sum_level(0, l, x3)
+    sum_first(0)
+    sum_fourth(1)
+
+    pair_inputs(0)
+    sum_second(0)
+    conv(0, wide, 0, g3, y1, -1)
+    features_out(0)
+    sum_fifth(1)
+    pair_gradient(0)
+    sum_third(0)
     grad_next(0)
-
-    def features_out(l):
-        if W[l] < 128:
-            v = jnp.where(masks[l][1:2, :] > 0, y1[l][...] + xf[l][...], 0.0)
-            gfeat[l][...] = pltpu.roll(v, NP[l] - W[l], 1).T[0 : N[l]].astype(BF16)
-            return
-
-        def body(r0, rc, lanes):
-            for r in range(R[l]):
-                for h in range(halves(l)):
-                    a = (r + 1) * W[l] + 128 * h
-                    m = masks[l][1:2, a : a + 128] > 0
-                    v = y1[l][pl.ds(r0, rc), a : a + 128] + xf[l][pl.ds(r0, rc), a : a + 128]
-                    stage[h, pl.ds(r0 * R[l] + r, rc, stride=R[l]), :] = jnp.where(m, v, 0.0)
-
-        each(l, body)
-        for h in range(halves(l)):
-            gfeat[l][:, 128 * h : 128 * h + 128] = stage[h].astype(BF16)
-
-    for l in (0, 1):
-        conv(l, wide, 0, g3, y1, -1)
-        features_out(l)
-    sum_second(0)
-    sum_third(1)
+    conv(1, wide, 0, g3, y1, -1)
+    features_out(1)
+    sum_sixth(1)
+    sum_fourth(0)
     for l in (2, 3):
         conv(l, wide, 0, g3, y1, -1)
         features_out(l)
-    sum_fourth(1)
-    sum_third(0)
+    grad_third(0)
+    sum_fifth(0)
+    coarse_inputs(1)
+    coarse_gradient(1)
+    sum_sixth(0)
+    coarse_inputs(0)
     coarse_gradient(0)
-    sum_fourth(0)
     sum_last(1)
     sum_last(0)
     for c in range(2):
@@ -1325,7 +1523,7 @@
     for l in range(LEVELS):
         n = C[l] // nb
         for c in range(2):
-            if l in sz.sum_levels:
+            if (l, 0) in sz.spots:
                 parts = []
                 for i in range(-(-3 * C[l] // 128)):
                     at, rows = sz.spots[l, i]
@@ -1333,7 +1531,7 @@
                 v = jnp.concatenate(parts, axis=1)
             for t in range(3):
                 for u in range(3):
-                    if l in sz.sum_levels:
+                    if (l, 0) in sz.spots:
                         kernels[l][c, t, u] = v[t * n : (t + 1) * n, u * C[l] : (u + 1) * C[l]]
                     else:
                         kernels[l][c, t, u] = coarse[c, t * n : (t + 1) * n, u * C[l] : (u + 1) * C[l]]
@@ -1383,7 +1581,7 @@
     map_shapes = [(C[0] * R[0], W[0])]
     map_shapes += [(C[l] * R[l], W[l]) if W[l] >= 128 else (N[l], C[l]) for l in range(4)]
     outs = [shape(m, BF16) for m in map_shapes]
-    outs += [shape((2, nk, sz.part, 128), BF16)]
+    outs += [shape((2, sz.sum_rows, 128), BF16)]
     outs += [shape((2, 3 * C[3] // nb if sz.gather else 3 * C[3], 3 * C[3]), F32)]
     outs += [shape((3, 16, 128), F32)]
     vm = pltpu.VMEM
@@ -1419,46 +1617,64 @@
     scratch += [vm((8, NP[l]), F32) for l in range(4)]
     mid = sum(max(2 * W[l], 128) for l in range(1, 4)) + W[0]
     scratch += [
-        vm((6, nb, 16, 128), F32),
-        vm((6, nk, 16, 128), F32),
+        vm((10, nb, 16, 128), F32),
+        vm((10, nk, 16, 128), F32),
         vm((2, sz.rim_total, 128), BF16),
         vm((4, 2, sz.rim_total, 128), BF16),
         vm((2, sz.uchan, mid), BF16),
         vm((2, sz.uchan, mid), BF16),
-        pltpu.SemaphoreType.DMA((6, nb)),
-        pltpu.SemaphoreType.DMA((6, nb)),
-        pltpu.SemaphoreType.DMA((6, nk)),
-        pltpu.SemaphoreType.DMA((6, nk)),
-        pltpu.SemaphoreType.DMA((5, 2)),
-        pltpu.SemaphoreType.DMA((5, 2)),
+        pltpu.SemaphoreType.DMA((10, nb)),
+        pltpu.SemaphoreType.DMA((10, nb)),
+        pltpu.SemaphoreType.DMA((10, nk)),
+        pltpu.SemaphoreType.DMA((10, nk)),
+        pltpu.SemaphoreType.DMA((9, 2)),
+        pltpu.SemaphoreType.DMA((9, 2)),
         pltpu.SemaphoreType.DMA((4, 2)),
         pltpu.SemaphoreType.DMA((2, 9)),
         vm((8, sz.blocks * 128), F32),
         vm((8, sz.ublocks * 128), F32),
-        vm((2, sz.nc, sz.ny, sz.sum_rows, 128), BF16),
-        vm((2, sz.ny, sz.sum_rows, 128), BF16),
-        vm((2, sz.ny, sz.sum_rows, 128), BF16),
-        vm((2, nk, sz.part, 128), BF16),
-        vm((2, nk, sz.part, 128), BF16),
+        vm((2, sz.nc, sz.ny, sz.batch_rows, 128), BF16),
+        vm((2, sz.ny, sz.batch_rows, 128), BF16),
+        vm((2, sz.ny, sz.batch_rows, 128), BF16),
+        vm((2, sz.sum_rows, 128), BF16),
+        vm((2, sz.nz * sz.part, 128), BF16),
+        vm((2, sz.nz, sz.part, 128), BF16),
+        vm((2, sz.sum_rows, 128), BF16),
         pltpu.SemaphoreType.DMA((2,)),
     ]
     sems = pltpu.SemaphoreType.DMA
-    scratch += [sems((2,)), sems((2,))] + [sems((2, sz.ny))] * 2 + [sems((2, nk))] * 4
+    scratch += [sems((2,))] * 2 + [sems((2, sz.ny))] * 2 + [sems((2,))] * 2 + [sems((2, sz.nz))] * 4
+    scratch += [sems((2,))] * 2
     if sz.gather:
         half = C[3] // nb // 2
         most = max(sz.nz, sz.nx, sz.ny, sz.nc)
         scratch += [
             vm((2, sz.nc, sz.ny, sz.nx, sz.nz, C[3] // 2, 128), BF16),
             vm((2, nb, half, 128), BF16),
-            vm((2, nk, nb, half, 128), BF16),
+            vm((2, sz.nx, sz.nz, nb, half, 128), BF16),
             vm((max(3, nb), 3 * C[3], max(C[3], 128 * sz.nz)), BF16),
             vm((nb, 3 * C[3] // nb, 128 * sz.nz), BF16),
             sems((2, 4, most)),
             sems((2, 4, most)),
             sems((2, nb)),
             sems((2, nb)),
-            sems((2, nk)),
-            sems((2, nk)),
+            sems((2, sz.nz)),
+            sems((2, sz.nz)),
+            sems((2,)),
+            sems((2,)),
+        ]
+    if sz.pair:
+        c2 = C[2] // nb
+        scratch += [
+            vm((2, sz.nc, sz.ny, C[2], NP[2]), BF16),
+            vm((nb, 3 * C[2], NP[2]), BF16),
+            vm((2, nb, c2, N[2]), BF16),
+            vm((2, nb, c2, N[2]), BF16),
+            vm((nb, 3 * c2, NP[2]), BF16),
+            sems((2, 2, max(sz.ny, sz.nc))),
+            sems((2, 2, max(sz.ny, sz.nc))),
+            sems((2, nb)),
+            sems((2, nb)),
         ]
     in_vmem = pl.BlockSpec(memory_space=pltpu.VMEM)
     in_smem = pl.BlockSpec(memory_space=pltpu.SMEM)
@@ -1497,7 +1713,7 @@
         out_specs=[in_any] * 5 + [in_vmem] * (len(outs) - 5),
         scratch_shapes=[pltpu.SemaphoreType.DMA((5,))],
         compiler_params=pltpu.CompilerParams(vmem_limit_bytes=60 * 2**20),
-    )(*maps, sums.reshape(2, sz.sum_rows, 128), totals, coarse)
+    )(*maps, sums, totals, coarse)
     shaped = []
     for i, m in enumerate(outs[0:5]):
         l = max(i - 1, 0)

time: 163 us -> 141 us (0.87)
  Pallas kernels: 160 us -> 138 us
    pallas_call x1, Pallas kernels: 155 us -> 133 us  [body(): pl.pallas_call(functools.partial(main_kernel, sz, nb, nk), out_shape=outs...]
where the time goes in v1:
time: 141 us; the launch traced here: 140 us
  Pallas kernels  138 us (98%)
  local copies, waits for them, and re-layouts  1.61 us (1%)
    pallas_call x1, Pallas kernels, body(): pl.pallas_call(functools.partial(main_kernel, sz, nb, nk), out_shape=outs...  133 us
    pallas_call x1, Pallas kernels, body(): pl.pallas_call(functools.partial(last_kernel, sz, nb), out_shape=outs, in...  5.3 us

profile of v1, /device:TPU:0, one launch (start us, length us, event | category | flops | bytes accessed | tf_op | source)
XLA Modules:
  0.0 140.4 jit_solution(7652150208817457197)
XLA Ops:
  0.7 132.8 %shard_map.360 = (bf16[768,256]{1,0:T(8,128)(2,1)}, bf16[768,256]{1,0:T(8,128)(2,1)}, bf16[768,128]{1,0:T(8,128)(2,1)}, bf16[256,192]{1,0:T(8,128)(2,1)}, bf16[6...) custom-call(s32[4]{0:T(128)} %refs_0_.1, s32[4]{0:T(128)} %refs_1_.1, ...), custom_call_target="tpu_custom_call" | custom-call | tf_op jit(solution)/shard_map/pallas_call | solution.py:1681
  133.5 5.3 %shard_map.361 = (bf16[768,256]{1,0:T(8,128)(2,1)}, bf16[768,256]{1,0:T(8,128)(2,1)}, bf16[768,128]{1,0:T(8,128)(2,1)}, bf16[256,192]{1,0:T(8,128)(2,1)}, bf16[6...) custom-call(bf16[768,256]{1,0:T(8,128)(2,1)} %get-tuple-element.40.r, ...), custom_call_target="tpu_custom_call" | custom-call | tf_op jit(solution)/shard_map/pallas_call | solution.py:1709
  138.8 1.6 %copy.41 = f32[2,3,3,12,48]{4,0,3,2,1:T(2,128)} copy(f32[2,3,3,12,48]{4,3,2,1,0:T(8,128)} %get-tuple-element.69) | data formatting | bytes 82944

commit v2 on v1

--- a/solution.py
+++ b/solution.py
@@ -45,7 +45,7 @@
         self.ny = nb // self.nc
         self.nz = nk // self.nx
         self.gather = nb * nk <= 32 and self.nx == 2 and self.nc == 2 and self.own[3] == 64
-        self.pair = self.gather and self.chan[2] // nb % 16 == 0 and self.own[2] % 128 == 0
+        self.pair = self.gather and self.chan[2] // nb % 16 == 0 and self.chan[2] % 128 == 64
         self.sum_levels = [0, 1] if self.pair else [0, 1, 2]
         self.stacked = [l for l in range(3 if self.gather else 4) if self.width[l] < 128]
         self.stacked = [l for l in self.stacked if not (self.pair and l == 2)]
@@ -59,13 +59,21 @@
                 self.spots[(*key, i)] = (at, rows)
                 at += rows
 
-        for l in self.sum_levels:
-            place((l,), 3 * self.chan[l] // nb, 3 * self.chan[l])
+        place((0,), 3 * self.chan[0] // nb, 3 * self.chan[0])
         for j in range(3):
             place(("u", j), self.uchan // nb, self.chan[j + 1])
+        self.early_rows = at
+        for l in self.sum_levels[1:]:
+            place((l,), 3 * self.chan[l] // nb, 3 * self.chan[l])
         self.batch_rows = at
         if self.pair:
-            place((2,), 3 * self.chan[2] // nb, 3 * self.chan[2])
+            rows = 9 * self.chan[2] // nb
+            for i in range(self.chan[2] // 128):
+                self.spots[2, i] = (at, rows)
+                at += rows
+            rows = -(-rows // 32) * 16
+            self.spots[2, self.chan[2] // 128] = (at, rows)
+            at += rows
         self.part = -(-at // (nk * 16)) * 16
         self.sum_rows = self.part * nk
 
@@ -138,14 +146,14 @@
     (sa_send, sa_recv, sb_send, sb_recv, rim_send, rim_recv) = take(6)
     raw_sem, wide_sem = take(2)
     prow, urow = take(2)
-    part_a, got_a, got_b, part_s, got_x, got_z, got_d, out_sem = take(8)
-    (ra_send, ra_recv, rb_send, rb_recv, rx_send, rx_recv, rz_send, rz_recv) = take(8)
+    part_a, got_a, part_s, got_x, got_z, got_d, out_sem = take(7)
+    (ra_send, ra_recv, rx_send, rx_recv, rz_send, rz_recv) = take(6)
     (dz_send, dz_recv, dx_send, dx_recv) = take(4)
     if sz.gather:
-        xg, gs, gr, x3g, t3g = take(5)
+        xg, xi, gs, gr, g9 = take(5)
         (xg_send, xg_recv, g1_send, g1_recv, g2_send, g2_recv, g3_send, g3_recv) = take(8)
     if sz.pair:
-        xb, x3b, gsb, gb, t3b = take(5)
+        xb, gsb, gb, g9b = take(4)
         (xb_send, xb_recv, gb_send, gb_recv) = take(4)
 
     C, R, W, N, NP, OFF = sz.chan, sz.rows, sz.width, sz.own, sz.flat, sz.off
@@ -160,7 +168,7 @@
 
     def raw_copy(l, which):
         if l == 3 and sz.gather:
-            dst = x3g.at[0:3, :, 0 : C[3]]
+            dst = g9.at[:, :, 0 : C[3]]
         else:
             dst = raw[l]
         return pltpu.make_async_copy(blocks[l].at[which], dst, raw_sem.at[l, which])
@@ -200,7 +208,7 @@
         for l in range(LEVELS):
             for t in range(3):
                 if l == 3 and sz.gather:
-                    v = x3g[t, :, 0 : C[3]]
+                    v = g9[t, :, 0 : C[3]]
                 else:
                     v = raw[l][t]
                 wide[l][which, t * C[l] : (t + 1) * C[l], :] = v.T
@@ -515,7 +523,8 @@
             body(pl.multiple_of(i * rc, rc), rc, lanes)
             return 0
 
-        lax.fori_loop(0, C[l] // rc, step, 0)
+        count = C[l] // rc
+        lax.fori_loop(0, count, step, 0, unroll=max(k for k in range(1, 9) if count % k == 0))
 
     def lane_chunks(l, lanes):
         return [(i, i + lanes) for i in range(0, NP[l], lanes)]
@@ -552,7 +561,7 @@
 
             lax.fori_loop(0, N[l] // span, step, 0)
         else:
-            rows = 96
+            rows = c if c <= 384 else 96
 
             def step(i, _):
                 acc = None
@@ -604,7 +613,7 @@
     def sum_pack(c, l):
         n = C[l] // nb
         for q in range(nb):
-            dst = part_a.at[c, q % nc, q // nc]
+            dst = part_a.at[c, q]
             for i in range(-(-3 * C[l] // 128)):
                 at, rows = sz.spots[l, i]
                 lanes = slice(128 * i, 128 * i + 128)
@@ -616,7 +625,7 @@
     def sum_pack_unites():
         n = sz.uchan // nb
         for q in range(nb):
-            dst = part_a.at[1, q % nc, q // nc]
+            dst = part_a.at[1, q]
             for j in range(3):
                 for i in range(-(-C[j + 1] // 128)):
                     at, rows = sz.spots["u", j, i]
@@ -625,22 +634,14 @@
                         v = jnp.concatenate([v, jnp.zeros((rows - n, 128), F32)], axis=0)
                     dst[at : at + rows, :] = v.astype(BF16)
 
-    def core_copies(c):
+    def batch_copies(c, part, sending):
+        rows = (slice(0, sz.early_rows), slice(sz.early_rows, sz.batch_rows))[part]
         out = []
-        for other in others(nc, my_core):
-            target = (my_y * nc + other, me_k)
-            out.append(remote(part_a.at[c, other], got_a.at[c], ra_send.at[c], ra_recv.at[c], target))
-        return out
-
-    def y_copies(c, sending):
-        out = []
-        for other in others(ny, my_y):
-            target = (other * nc + my_core, me_k)
-            if sending:
-                src, dst, sem = part_a.at[c, my_core, other], got_b.at[c, my_y], rb_recv.at[c, my_y]
-            else:
-                src, dst, sem = part_a.at[c, my_core, other], got_b.at[c, other], rb_recv.at[c, other]
-            out.append(remote(src, dst, rb_send.at[c, other], sem, target))
+        for other in others(nb, me_b):
+            slot = me_b if sending else other
+            src, dst = part_a.at[c, other, rows, :], got_a.at[c, slot, rows, :]
+            sems = ra_send.at[c, part, other], ra_recv.at[c, part, slot]
+            out.append(remote(src, dst, *sems, (other, me_k)))
         return out
 
     def part_at(x, z, n=1):
@@ -692,32 +693,22 @@
         kernel_grad(l, src)
         sum_pack(c, l)
 
-    def sum_first(c):
-        for copy in core_copies(c):
+    def sum_first(c, part):
+        for copy in batch_copies(c, part, True):
             copy.start()
 
     def sum_second(c):
-        copies = core_copies(c)
-        finish((copies, copies))
-        for y in range(ny):
-            v = part_a[c, my_core, y].astype(F32)
-            if nc > 1:
-                v = v + got_a[c, y].astype(F32)
-            part_a[c, my_core, y] = v.astype(BF16)
-        for copy in y_copies(c, True):
-            copy.start()
-
-    def sum_third(c):
-        finish((y_copies(c, True), y_copies(c, False)))
-        got_b[c, my_y] = part_a[c, my_core, my_y]
-        v = got_b[c, 0].astype(F32)
-        for y in range(1, ny):
-            v = v + got_b[c, y].astype(F32)
+        for part in range(2):
+            finish((batch_copies(c, part, True), batch_copies(c, part, False)))
+        got_a[c, me_b] = part_a[c, me_b]
+        v = got_a[c, 0].astype(F32)
+        for b in range(1, nb):
+            v = v + got_a[c, b].astype(F32)
         part_s[c, 0 : sz.batch_rows, :] = v.astype(BF16)
         for copy in x_copies(c):
             copy.start()
 
-    def sum_fourth(c):
+    def sum_third(c):
         copies = x_copies(c)
         finish((copies, copies))
         mine = part_at(my_x, 0, nz)
@@ -727,7 +718,7 @@
         for copy in z_copies(c, True):
             copy.start()
 
-    def sum_fifth(c):
+    def sum_fourth(c):
         finish((z_copies(c, True), z_copies(c, False)))
         got_z[c, my_z] = part_s[c, part_at(my_x, my_z), :]
         v = got_z[c, 0].astype(F32)
@@ -737,7 +728,7 @@
         for copy in back_z_copies(c, True):
             copy.start()
 
-    def sum_sixth(c):
+    def sum_fifth(c):
         finish((back_z_copies(c, True), back_z_copies(c, False)))
         for copy in back_x_copies(c, True):
             copy.start()
@@ -773,27 +764,6 @@
         for copy in pair_copies(c, 1, True):
             copy.start()
 
-    def pair_inputs(c):
-        if not sz.pair:
-            return
-        finish((pair_copies(c, 1, True), pair_copies(c, 1, False)))
-        at = lax.broadcasted_iota(jnp.int32, (1, NP[2]), 1) & (W[2] - 1)
-
-        def item(b, _):
-            def group(q, _):
-                rows = pl.ds(pl.multiple_of(q * c2, 16), c2)
-                v = xb[c, lax.rem(b, nc), lax.div(b, nc), rows, :].astype(F32)
-                left = jnp.where(at == 0, 0.0, pltpu.roll(v, 1, 1))
-                right = jnp.where(at == W[2] - 1, 0.0, pltpu.roll(v, NP[2] - 1, 1))
-                for u, part in enumerate((left, v, right)):
-                    x3b[b, pl.ds(pl.multiple_of(u * C[2] + q * c2, 16), c2), :] = part.astype(BF16)
-                return 0
-
-            lax.fori_loop(0, nb, group, 0)
-            return 0
-
-        lax.fori_loop(0, nb, item, 0)
-
     def pair_grad_copies(c, sending):
         out = []
         for other in others(nb, me_b):
@@ -811,28 +781,50 @@
             for copy in pair_grad_copies(c, True):
                 copy.start()
 
+    def nine_shifts(v, width, store):
+        lanes = v.shape[1]
+        lane = lax.broadcasted_iota(jnp.int32, (1, lanes), 1)
+        at = lane & (width - 1)
+        left = jnp.where(at == width - 1, 0.0, pltpu.roll(v, lanes - 1, 1))
+        right = jnp.where(at == 0, 0.0, pltpu.roll(v, 1, 1))
+        for u, part in enumerate((left, v, right)):
+            store(0, u, jnp.where(lane >= lanes - width, 0.0, pltpu.roll(part, lanes - width, 1)))
+            store(1, u, part)
+            store(2, u, jnp.where(lane < width, 0.0, pltpu.roll(part, width, 1)))
+
     def pair_gradient(c):
         if not sz.pair:
             return
+        finish((pair_copies(c, 1, True), pair_copies(c, 1, False)))
         finish((pair_grad_copies(c, True), pair_grad_copies(c, False)))
         gb[c, me_b] = gsb[c, me_b]
 
         def item(b, _):
             v = jnp.concatenate([gb[c, b].astype(F32), jnp.zeros((c2, NP[2] - N[2]), F32)], axis=1)
-            for t in range(3):
-                part = pltpu.roll(v, t * W[2], 1) if t else v
-                t3b[b, t * c2 : (t + 1) * c2, :] = part.astype(BF16)
+
+            def store(t, u, part):
+                at = (3 * t + u) * c2
+                g9b[b, at : at + c2, :] = part.astype(BF16)
+
+            nine_shifts(pltpu.roll(v, W[2], 1), W[2], store)
             return 0
 
         lax.fori_loop(0, nb, item, 0)
         acc = None
         for b in range(nb):
-            part = lax.dot_general(t3b[b], x3b[b], (((1,), (1,)), ((), ())), preferred_element_type=F32)
+            part = lax.dot_general(
+                g9b[b], xb[c, b % nc, b // nc], (((1,), (1,)), ((), ())), preferred_element_type=F32
+            )
             acc = part if acc is None else acc + part
-        for i in range(-(-3 * C[2] // 128)):
+        whole = C[2] // 128
+        for i in range(whole):
             at, rows = sz.spots[2, i]
-            m = min(128, 3 * C[2] - 128 * i)
-            part_s[c, at : at + rows, 0:m] = acc[:, 128 * i : 128 * i + m].astype(BF16)
+            part_s[c, at : at + rows, :] = acc[:, 128 * i : 128 * i + 128].astype(BF16)
+        at, rows = sz.spots[2, whole]
+        rest = acc[:, 128 * whole :]
+        low, high = rest[0:rows], rest[rows:]
+        high = jnp.concatenate([high, jnp.zeros((rows - high.shape[0], high.shape[1]), F32)], axis=0)
+        part_s[c, at : at + rows, :] = jnp.concatenate([low, high], axis=1).astype(BF16)
 
     c3 = C[3] // nb
     half = c3 // 2
@@ -860,13 +852,13 @@
         for other in others(n, me):
             slot = me if sending else other
             if step == 0:
-                ref, target = xg.at[c, my_core, my_y, my_x, slot], (me_b, other * nx + my_x)
+                ref, target = xg.at[c, my_x, slot], (me_b, other * nx + my_x)
             elif step == 1:
-                ref, target = xg.at[c, my_core, my_y, slot], (me_b, my_z * nx + other)
+                ref, target = xg.at[c, slot], (me_b, my_z * nx + other)
             elif step == 2:
-                ref, target = xg.at[c, my_core, slot], (other * nc + my_core, me_k)
+                ref, target = xi.at[c, my_core, slot], (other * nc + my_core, me_k)
             else:
-                ref, target = xg.at[c, slot], (my_y * nc + other, me_k)
+                ref, target = xi.at[c, slot], (my_y * nc + other, me_k)
             out.append(remote(ref, ref, xg_send.at[c, step, other], xg_recv.at[c, step, slot], target))
         return out
 
@@ -879,11 +871,19 @@
 
     def gather_begin(c, ref):
         if sz.gather:
-            xg[c, my_core, my_y, my_x, my_z] = pack_pixels(ref[3])
+            xg[c, my_x, my_z] = pack_pixels(ref[3])
             gather_start(c, 0)
 
     def gather_next(c, step):
         gather_wait(c, step)
+        if step == 1 and sz.gather:
+            for z in range(nz):
+                for q in range(nb):
+                    rows = slice(q * half, (q + 1) * half)
+                    pair = unpack_pixels(xg[c, 0, z, rows, :], xg[c, 1, z, rows, :])
+                    for i, v in enumerate(pair):
+                        at = q * c3 + i * half
+                        xi[c, my_core, my_y, at : at + half, 128 * z : 128 * z + 128] = v.astype(BF16)
         gather_start(c, step + 1)
 
     def grad_copies(c, step, sending):
@@ -932,33 +932,9 @@
 
     image = nz * 128
 
-    def coarse_inputs(c):
-        if not sz.gather:
-            return
-        gather_wait(c, 3)
-        at = lane128 & (W[3] - 1)
-
-        def item(b, _):
-            def group(q, _):
-                for z in range(nz):
-                    rows = pl.ds(pl.multiple_of(q * half, 16), half)
-                    core, y = lax.rem(b, nc), lax.div(b, nc)
-                    pair = unpack_pixels(xg[c, core, y, 0, z, rows, :], xg[c, core, y, 1, z, rows, :])
-                    for i, v in enumerate(pair):
-                        left = jnp.where(at == 0, 0.0, pltpu.roll(v, 1, 1))
-                        right = jnp.where(at == W[3] - 1, 0.0, pltpu.roll(v, 127, 1))
-                        for u, part in enumerate((left, v, right)):
-                            spot = pl.ds(pl.multiple_of(u * C[3] + q * c3 + i * half, 16), half)
-                            x3g[b, spot, 128 * z : 128 * z + 128] = part.astype(BF16)
-                return 0
-
-            lax.fori_loop(0, nb, group, 0)
-            return 0
-
-        lax.fori_loop(0, nb, item, 0)
-
     def coarse_copy(c, i):
-        at = pl.ds(i * c3 if isinstance(i, int) else pl.multiple_of(i * c3, 16), c3)
+        n = 3 * c3
+        at = pl.ds(i * n if isinstance(i, int) else pl.multiple_of(i * n, 16), n)
         slot = i % 2 if isinstance(i, int) else lax.rem(i, 2)
         return pltpu.make_async_copy(cstage.at[slot], coarse_ref.at[c, at, :], cstage_sem.at[slot])
 
@@ -979,8 +955,8 @@
         if not sz.gather:
             coarse_local(c, a3 if c else x3)
             return
+        gather_wait(c, 3)
         finish((grad_copies(c, 2, True), grad_copies(c, 2, False)))
-        lane = lax.broadcasted_iota(jnp.int32, (1, image), 1)
 
         def item(b, _):
             low, high = [], []
@@ -989,22 +965,24 @@
                 low.append(first)
                 high.append(second)
             for i, parts in enumerate((low, high)):
-                v = jnp.concatenate(parts, axis=1) if nz > 1 else parts[0]
-                up_ = jnp.where(lane >= image - W[3], 0.0, pltpu.roll(v, image - W[3], 1))
-                down = jnp.where(lane < W[3], 0.0, pltpu.roll(v, W[3], 1))
-                for t, part in enumerate((up_, v, down)):
-                    spot = t * c3 + i * half
-                    t3g[b, spot : spot + half, :] = part.astype(BF16)
+
+                def store(t, u, part, i=i):
+                    spot = pl.ds(pl.multiple_of((3 * b + u) * c3 + i * half, 16), half)
+                    g9[t, spot, 0:image] = part.astype(BF16)
+
+                nine_shifts(jnp.concatenate(parts, axis=1) if nz > 1 else parts[0], W[3], store)
             return 0
 
         lax.fori_loop(0, nb, item, 0)
 
         def step(i, _):
-            at = pl.ds(pl.multiple_of(i * c3, 16), c3)
             acc = None
             for b in range(nb):
                 part = lax.dot_general(
-                    t3g[b, at, :], x3g[b, :, 0:image], (((1,), (1,)), ((), ())), preferred_element_type=F32
+                    g9[i, 3 * b * c3 : 3 * (b + 1) * c3, 0:image],
+                    xi[c, b % nc, b // nc],
+                    (((1,), (1,)), ((), ())),
+                    preferred_element_type=F32,
                 )
                 acc = part if acc is None else acc + part
             slot = lax.rem(i, 2)
@@ -1430,14 +1408,21 @@
     ex_start(8, record(stat_a, stat_b, spans_of[FINE]))
     sum_level(1, 0, a3)
     sum_pack_unites()
+    sum_first(1, 0)
     got = ex_end(7)
     totals_ref[1] = jnp.where(jnp.concatenate([fine_place] * 2, axis=0), got_f, got)
     norm_columns(rstd2_c * gain2_p, got, COARSE)
-    norm_grad(2, y2, xf)
+    norm_grad(1, y2, xf)
+    for l in sz.sum_levels[1:]:
+        if l == 2:
+            norm_grad(2, y2, xf)
+        sum_level(1, l, a3)
+    sum_first(1, 1)
+    if sz.pair:
+        norm_grad(2, y2, xf)
     pair_grad_begin(1)
     norm_grad(3, y2, xf)
     grad_begin(1)
-    norm_grad(1, y2, xf)
 
     for l in COARSE:
         conv(l, wide, 1, g3, p1, -1)
@@ -1445,60 +1430,55 @@
         first_sums(l)
     send_rims(3, COARSE, p1)
     ex_start(9, record(stat_a, stat_b, spans_of[COARSE]))
-    for l in sz.sum_levels[1:]:
-        sum_level(1, l, a3)
-    sum_first(1)
     ex_mid(8)
-    pair_inputs(1)
+    pair_gradient(1)
     ex_mid(9)
     sum_second(1)
     grad_next(1)
-    pair_gradient(1)
     gather_next(0, 2)
     gather_next(1, 2)
     got_f = ex_end(8)
     take_rims(3, FINE, p1)
     norm_columns(rstd1_f * gain1_p, got_f, FINE)
     norm_grad(0, y1, p1)
+    sum_level(0, 0, x3)
+    sum_first(0, 0)
     sum_third(1)
-    sum_level(0, 0, x3)
     grad_third(1)
     got = ex_end(9)
     totals_ref[2] = jnp.where(jnp.concatenate([fine_place] * 2, axis=0), got_f, got)
     take_rims(3, COARSE, p1)
     norm_columns(rstd1_c * gain1_p, got, COARSE)
-    norm_grad(2, y1, p1)
+    norm_grad(1, y1, p1)
+    for l in sz.sum_levels[1:]:
+        if l == 2:
+            norm_grad(2, y1, p1)
+        sum_level(0, l, x3)
+    sum_first(0, 1)
+    if sz.pair:
+        norm_grad(2, y1, p1)
     pair_grad_begin(0)
     norm_grad(3, y1, p1)
     grad_begin(0)
-    norm_grad(1, y1, p1)
-    for l in sz.sum_levels[1:]:
-        sum_level(0, l, x3)
-    sum_first(0)
     sum_fourth(1)
 
-    pair_inputs(0)
-    sum_second(0)
     conv(0, wide, 0, g3, y1, -1)
     features_out(0)
-    sum_fifth(1)
     pair_gradient(0)
-    sum_third(0)
+    sum_second(0)
     grad_next(0)
-    conv(1, wide, 0, g3, y1, -1)
-    features_out(1)
-    sum_sixth(1)
-    sum_fourth(0)
-    for l in (2, 3):
+    for l in (1, 2):
         conv(l, wide, 0, g3, y1, -1)
         features_out(l)
+    sum_fifth(1)
+    sum_third(0)
+    conv(3, wide, 0, g3, y1, -1)
+    features_out(3)
     grad_third(0)
+    coarse_gradient(1)
+    sum_fourth(0)
+    coarse_gradient(0)
     sum_fifth(0)
-    coarse_inputs(1)
-    coarse_gradient(1)
-    sum_sixth(0)
-    coarse_inputs(0)
-    coarse_gradient(0)
     sum_last(1)
     sum_last(0)
     for c in range(2):
@@ -1509,39 +1489,25 @@
     it = iter(refs)
     take = lambda n: [next(it) for _ in range(n)]
     maps = take(5)
-    sums, totals = take(2)
-    (coarse,) = take(1)
+    sums_in, totals, coarse_in = take(3)
     maps_out = take(5)
     kernels = take(4)
     unites = take(3)
     norm_gains, norm_shifts, unite_gains, unite_shifts = take(4)
-    (sem,) = take(1)
-    copies = [pltpu.make_async_copy(a, b, sem.at[i]) for i, (a, b) in enumerate(zip(maps, maps_out))]
-    for copy in copies:
+    held = take(5)
+    sums, coarse, in_sem, out_sem = take(4)
+    C = sz.chan
+    arrivals = [pltpu.make_async_copy(sums_in, sums, in_sem.at[0])]
+    arrivals += [pltpu.make_async_copy(a, b, in_sem.at[1 + i]) for i, (a, b) in enumerate(zip(maps, held))]
+    arrivals += [pltpu.make_async_copy(coarse_in.at[c], coarse.at[c], in_sem.at[6 + c]) for c in range(2)]
+    for copy in arrivals:
         copy.start()
-    C = sz.chan
-    for l in range(LEVELS):
-        n = C[l] // nb
-        for c in range(2):
-            if (l, 0) in sz.spots:
-                parts = []
-                for i in range(-(-3 * C[l] // 128)):
-                    at, rows = sz.spots[l, i]
-                    parts.append(sums[c, at : at + rows, :].astype(F32))
-                v = jnp.concatenate(parts, axis=1)
-            for t in range(3):
-                for u in range(3):
-                    if (l, 0) in sz.spots:
-                        kernels[l][c, t, u] = v[t * n : (t + 1) * n, u * C[l] : (u + 1) * C[l]]
-                    else:
-                        kernels[l][c, t, u] = coarse[c, t * n : (t + 1) * n, u * C[l] : (u + 1) * C[l]]
-    n = sz.uchan // nb
-    for j in range(3):
-        width = C[j + 1]
-        for i in range(-(-width // 128)):
-            at, _ = sz.spots["u", j, i]
-            m = min(128, width - 128 * i)
-            unites[j][:, 128 * i : 128 * i + m] = sums[1, at : at + n, 0:m].astype(F32)
+    leaving = [pltpu.make_async_copy(a, b, out_sem.at[i]) for i, (a, b) in enumerate(zip(held, maps_out))]
+    if sz.gather:
+        leaving += [
+            pltpu.make_async_copy(coarse.at[c], kernels[3].at[c], out_sem.at[5 + c]) for c in range(2)
+        ]
+
     for row, which in ((0, 2), (1, 1)):
         for k in range(sz.blocks):
             m = min(128, sz.total - 128 * k)
@@ -1551,7 +1517,57 @@
         v = jnp.concatenate([totals[0, base + k : base + k + 1, :] for k in range(sz.ublocks)], axis=1)
         for j in range(3):
             ref[j : j + 1, :] = v[:, j * sz.uchan : (j + 1) * sz.uchan]
-    for copy in copies:
+
+    arrivals[0].wait()
+    for i in range(5):
+        arrivals[1 + i].wait()
+        leaving[i].start()
+    for l in range(LEVELS):
+        n = C[l] // nb
+        if l == 3:
+            for c in range(2):
+                arrivals[6 + c].wait()
+                if sz.gather:
+                    leaving[5 + c].start()
+        for c in range(2):
+            if l == 2 and sz.pair:
+                at, rows = sz.spots[2, C[2] // 128]
+                block = sums[c, at : at + rows, :].astype(F32)
+                parts = []
+                for i in range(C[2] // 128):
+                    at, rows = sz.spots[2, i]
+                    parts.append(sums[c, at : at + rows, :].astype(F32))
+                parts.append(jnp.concatenate([block[:, 0:64], block[:, 64:128]], axis=0)[0 : 9 * n])
+                v = jnp.concatenate(parts, axis=1)
+            elif (l, 0) in sz.spots:
+                parts = []
+                for i in range(-(-3 * C[l] // 128)):
+                    at, rows = sz.spots[l, i]
+                    parts.append(sums[c, at : at + rows, :].astype(F32))
+                v = jnp.concatenate(parts, axis=1)
+            for t in range(3):
+                for u in range(3):
+                    at = (3 * t + u) * n
+                    if l == 3 and sz.gather:
+                        continue
+                    if l == 3:
+                        kernels[3][c, at : at + n, :] = coarse[c, t * n : (t + 1) * n, u * C[3] : (u + 1) * C[3]]
+                    elif l == 2 and sz.pair:
+                        kernels[2][c, t, u] = v[at : at + n]
+                    else:
+                        w = v[t * n : (t + 1) * n, u * C[l] : (u + 1) * C[l]]
+                        if l == 0:
+                            kernels[0][t, u, :, c, :] = w
+                        else:
+                            kernels[l][c, t, u] = w
+    n = sz.uchan // nb
+    for j in range(3):
+        width = C[j + 1]
+        for i in range(-(-width // 128)):
+            at, _ = sz.spots["u", j, i]
+            m = min(128, width - 128 * i)
+            unites[j][:, 128 * i : 128 * i + m] = sums[1, at : at + n, 0:m].astype(F32)
+    for copy in leaving:
         copy.wait()
 
 
@@ -1582,7 +1598,7 @@
     map_shapes += [(C[l] * R[l], W[l]) if W[l] >= 128 else (N[l], C[l]) for l in range(4)]
     outs = [shape(m, BF16) for m in map_shapes]
     outs += [shape((2, sz.sum_rows, 128), BF16)]
-    outs += [shape((2, 3 * C[3] // nb if sz.gather else 3 * C[3], 3 * C[3]), F32)]
+    outs += [shape((2, 9 * C[3] // nb, C[3]) if sz.gather else (2, 3 * C[3], 3 * C[3]), F32)]
     outs += [shape((3, 16, 128), F32)]
     vm = pltpu.VMEM
     scratch = [
@@ -1593,7 +1609,8 @@
     for _ in range(3):
         scratch += [vm((3 * C[l], NP[l]), BF16) for l in range(4)]
     scratch += [vm((3 * C[l], NP[l]), BF16) for l in sz.stacked]
-    scratch += [vm((2, C[3] // nb, 3 * C[3]), F32), pltpu.SemaphoreType.DMA((2,))]
+    n = C[3] // nb
+    scratch += [vm((2, 3 * n, C[3]) if sz.gather else (1, n, 3 * C[3]), F32), pltpu.SemaphoreType.DMA((2,))]
     top = C[sz.sum_levels[-1]]
     scratch += [vm((3 * top, -(-3 * top // 128) * 128), F32)]
     scratch += [vm((sz.uchan, -(-C[l] // 128) * 128), F32) for l in range(1, 4)]
@@ -1633,9 +1650,8 @@
         pltpu.SemaphoreType.DMA((2, 9)),
         vm((8, sz.blocks * 128), F32),
         vm((8, sz.ublocks * 128), F32),
-        vm((2, sz.nc, sz.ny, sz.batch_rows, 128), BF16),
-        vm((2, sz.ny, sz.batch_rows, 128), BF16),
-        vm((2, sz.ny, sz.batch_rows, 128), BF16),
+        vm((2, nb, sz.batch_rows, 128), BF16),
+        vm((2, nb, sz.batch_rows, 128), BF16),
         vm((2, sz.sum_rows, 128), BF16),
         vm((2, sz.nz * sz.part, 128), BF16),
         vm((2, sz.nz, sz.part, 128), BF16),
@@ -1643,17 +1659,17 @@
         pltpu.SemaphoreType.DMA((2,)),
     ]
     sems = pltpu.SemaphoreType.DMA
-    scratch += [sems((2,))] * 2 + [sems((2, sz.ny))] * 2 + [sems((2,))] * 2 + [sems((2, sz.nz))] * 4
+    scratch += [sems((2, 2, nb))] * 2 + [sems((2,))] * 2 + [sems((2, sz.nz))] * 4
     scratch += [sems((2,))] * 2
     if sz.gather:
         half = C[3] // nb // 2
         most = max(sz.nz, sz.nx, sz.ny, sz.nc)
         scratch += [
-            vm((2, sz.nc, sz.ny, sz.nx, sz.nz, C[3] // 2, 128), BF16),
+            vm((2, sz.nx, sz.nz, C[3] // 2, 128), BF16),
+            vm((2, sz.nc, sz.ny, C[3], 128 * sz.nz), BF16),
             vm((2, nb, half, 128), BF16),
             vm((2, sz.nx, sz.nz, nb, half, 128), BF16),
-            vm((max(3, nb), 3 * C[3], max(C[3], 128 * sz.nz)), BF16),
-            vm((nb, 3 * C[3] // nb, 128 * sz.nz), BF16),
+            vm((3, 3 * C[3], max(C[3], 128 * sz.nz)), BF16),
             sems((2, 4, most)),
             sems((2, 4, most)),
             sems((2, nb)),
@@ -1667,10 +1683,9 @@
         c2 = C[2] // nb
         scratch += [
             vm((2, sz.nc, sz.ny, C[2], NP[2]), BF16),
-            vm((nb, 3 * C[2], NP[2]), BF16),
             vm((2, nb, c2, N[2]), BF16),
             vm((2, nb, c2, N[2]), BF16),
-            vm((nb, 3 * c2, NP[2]), BF16),
+            vm((nb, 9 * c2, NP[2]), BF16),
             sems((2, 2, max(sz.ny, sz.nc))),
             sems((2, 2, max(sz.ny, sz.nc))),
             sems((2, nb)),
@@ -1703,17 +1718,31 @@
         coarse = coarse.astype(F32).reshape(2, 3 * C[3] // nb, 3 * C[3])
     in_any = pl.BlockSpec(memory_space=pl.ANY)
     outs = [shape(m, BF16) for m in map_shapes]
-    outs += [shape((2, 3, 3, C[l] // nb, C[l]), F32) for l in range(4)]
+    outs += [shape((3, 3, C[0] // nb, 2, C[0]), F32)]
+    outs += [shape((2, 3, 3, C[l] // nb, C[l]), F32) for l in (1, 2)]
+    outs += [shape((2, 9 * C[3] // nb, C[3]), F32)]
     outs += [shape((sz.uchan // nb, C[l]), F32) for l in range(1, 4)]
     outs += [shape((2, sz.total), F32)] * 2 + [shape((3, sz.uchan), F32)] * 2
     outs = pl.pallas_call(
         functools.partial(last_kernel, sz, nb),
         out_shape=outs,
-        in_specs=[in_vmem] * 8,
-        out_specs=[in_any] * 5 + [in_vmem] * (len(outs) - 5),
-        scratch_shapes=[pltpu.SemaphoreType.DMA((5,))],
+        in_specs=[in_any] * 6 + [in_vmem] + [in_any],
+        out_specs=[in_any] * 5
+        + [in_vmem] * 3
+        + [in_any if sz.gather else in_vmem]
+        + [in_vmem] * (len(outs) - 9),
+        scratch_shapes=[vm(m, BF16) for m in map_shapes]
+        + [
+            vm(sums.shape, BF16),
+            vm(coarse.shape, F32),
+            pltpu.SemaphoreType.DMA((8,)),
+            pltpu.SemaphoreType.DMA((7,)),
+        ],
         compiler_params=pltpu.CompilerParams(vmem_limit_bytes=60 * 2**20),
     )(*maps, sums, totals, coarse)
+    outs = list(outs)
+    outs[5] = outs[5].transpose(3, 0, 1, 2, 4)
+    outs[8] = outs[8].reshape(2, 3, 3, C[3] // nb, C[3])
     shaped = []
     for i, m in enumerate(outs[0:5]):
         l = max(i - 1, 0)

time: 141 us -> 122 us (0.87)
  Pallas kernels: 138 us -> 121 us
  local copies, waits for them, and re-layouts: 1.61 us -> 0 us
    pallas_call x1, Pallas kernels: 133 us -> 115 us  [body(): pl.pallas_call(functools.partial(main_kernel, sz, nb, nk), out_shape=outs...]
    unnamed x1 -> x0, local copies, waits for them, and re-layouts: 1.61 us -> none
where the time goes in v2:
time: 122 us
  Pallas kernels  121 us (99%)
    pallas_call x1, Pallas kernels, body(): pl.pallas_call(functools.partial(main_kernel, sz, nb, nk), out_shape=outs...  115 us
    pallas_call x1, Pallas kernels, body(): pl.pallas_call(functools.partial(last_kernel, sz, nb), out_shape=outs, in...  5.59 us

profile of v2, /device:TPU:0, one launch (start us, length us, event | category | flops | bytes accessed | tf_op | source)
XLA Modules:
  0.0 121.9 jit_solution(11471938395435365197)
XLA Ops:
  0.7 115.4 %shard_map.360 = (bf16[768,256]{1,0:T(8,128)(2,1)}, bf16[768,256]{1,0:T(8,128)(2,1)}, bf16[768,128]{1,0:T(8,128)(2,1)}, bf16[256,192]{1,0:T(8,128)(2,1)}, bf16[6...) custom-call(s32[4]{0:T(128)} %refs_0_.1, s32[4]{0:T(128)} %refs_1_.1, ...), custom_call_target="tpu_custom_call" | custom-call | tf_op jit(solution)/shard_map/pallas_call | solution.py:1696
  116.1 5.6 %shard_map.361 = (bf16[768,256]{1,0:T(8,128)(2,1)}, bf16[768,256]{1,0:T(8,128)(2,1)}, bf16[768,128]{1,0:T(8,128)(2,1)}, bf16[256,192]{1,0:T(8,128)(2,1)}, bf16[6...) custom-call(bf16[768,256]{1,0:T(8,128)(2,1)} %get-tuple-element.40.r, ...), custom_call_target="tpu_custom_call" | custom-call | tf_op jit(solution)/shard_map/pallas_call | solution.py:1726

commit v3 on v2

--- a/solution.py
+++ b/solution.py
@@ -49,23 +49,30 @@
         self.sum_levels = [0, 1] if self.pair else [0, 1, 2]
         self.stacked = [l for l in range(3 if self.gather else 4) if self.width[l] < 128]
         self.stacked = [l for l in self.stacked if not (self.pair and l == 2)]
-        self.spots = {}
-        at = 0
-
-        def place(key, values, width):
-            nonlocal at
+        self.start, self.spots, self.moves = {}, {}, []
+
+        def place(table, at, key, values, width):
             rows = -(-values // 16) * 16
             for i in range(-(-width // 128)):
-                self.spots[(*key, i)] = (at, rows)
+                table[(*key, i)] = (at, rows)
                 at += rows
-
-        place((0,), 3 * self.chan[0] // nb, 3 * self.chan[0])
-        for j in range(3):
-            place(("u", j), self.uchan // nb, self.chan[j + 1])
-        self.early_rows = at
-        for l in self.sum_levels[1:]:
-            place((l,), 3 * self.chan[l] // nb, 3 * self.chan[l])
-        self.batch_rows = at
+            return at
+
+        def place_kernels(table, at, levels):
+            for l in levels:
+                at = place(table, at, (l,), 3 * self.chan[l] // nb, 3 * self.chan[l])
+            return at
+
+        def place_unites(table, at):
+            for j in range(3):
+                at = place(table, at, ("u", j), self.uchan // nb, self.chan[j + 1])
+            return at
+
+        ends = [0, place_kernels(self.start, 0, [0])]
+        ends.append(place_unites(self.start, ends[-1]))
+        ends.append(place_kernels(self.start, ends[-1], self.sum_levels[1:]))
+        self.early_rows, self.batch_rows = ends[2], ends[3]
+        at = place_kernels(self.spots, 0, self.sum_levels)
         if self.pair:
             rows = 9 * self.chan[2] // nb
             for i in range(self.chan[2] // 128):
@@ -74,8 +81,11 @@
             rows = -(-rows // 32) * 16
             self.spots[2, self.chan[2] // 128] = (at, rows)
             at += rows
-        self.part = -(-at // (nk * 16)) * 16
-        self.sum_rows = self.part * nk
+        rows_of = [at, place_unites(self.spots, at)]
+        self.part = [-(-r // (nk * 16)) * 16 for r in rows_of]
+        self.sum_rows = max(self.part) * nk
+        kernels_end = ends[3] - ends[2]
+        self.moves = [(0, 0, ends[1]), (ends[2], ends[1], kernels_end), (ends[1], at, ends[2] - ends[1])]
 
 
 def blend(scale, rows):
@@ -546,7 +556,7 @@
     def conv(l, w, which, src, dst, sign=1):
         c = C[l]
         if W[l] % 128 == 0:
-            span = min(1024, N[l])
+            span = min(2048, N[l])
 
             def step(i, _):
                 acc = None
@@ -615,7 +625,7 @@
         for q in range(nb):
             dst = part_a.at[c, q]
             for i in range(-(-3 * C[l] // 128)):
-                at, rows = sz.spots[l, i]
+                at, rows = sz.start[l, i]
                 lanes = slice(128 * i, 128 * i + 128)
                 parts = [kg[t * C[l] + q * n : t * C[l] + q * n + n, lanes] for t in range(3)]
                 if rows > 3 * n:
@@ -628,7 +638,7 @@
             dst = part_a.at[1, q]
             for j in range(3):
                 for i in range(-(-C[j + 1] // 128)):
-                    at, rows = sz.spots["u", j, i]
+                    at, rows = sz.start["u", j, i]
                     v = gun[j][q * n : q * n + n, 128 * i : 128 * i + 128]
                     if rows > n:
                         v = jnp.concatenate([v, jnp.zeros((rows - n, 128), F32)], axis=0)
@@ -644,31 +654,31 @@
             out.append(remote(src, dst, *sems, (other, me_k)))
         return out
 
-    def part_at(x, z, n=1):
-        return pl.ds(pl.multiple_of((x * nz + z) * sz.part, 16), n * sz.part)
+    def part_at(c, x, z, n=1):
+        return pl.ds(pl.multiple_of((x * nz + z) * sz.part[c], 16), n * sz.part[c])
 
     def x_copies(c):
         out = []
         for other in others(nx, my_x):
-            src = part_s.at[c, part_at(other, 0, nz), :]
+            src = part_s.at[c, part_at(c, other, 0, nz), :]
             target = (me_b, my_z * nx + other)
-            out.append(remote(src, got_x.at[c], rx_send.at[c], rx_recv.at[c], target))
+            out.append(remote(src, got_x.at[c, 0 : nz * sz.part[c], :], rx_send.at[c], rx_recv.at[c], target))
         return out
 
     def z_copies(c, sending):
         out = []
         for other in others(nz, my_z):
             slot = my_z if sending else other
-            src = part_s.at[c, part_at(my_x, other), :]
+            src = part_s.at[c, part_at(c, my_x, other), :]
             target = (me_b, other * nx + my_x)
-            out.append(remote(src, got_z.at[c, slot], rz_send.at[c, other], rz_recv.at[c, slot], target))
+            out.append(remote(src, got_z.at[c, slot, 0 : sz.part[c], :], rz_send.at[c, other], rz_recv.at[c, slot], target))
         return out
 
     def back_z_copies(c, sending):
         out = []
         for other in others(nz, my_z):
             slot = my_z if sending else other
-            src, dst = got_d.at[c, part_at(my_x, my_z), :], got_d.at[c, part_at(my_x, slot), :]
+            src, dst = got_d.at[c, part_at(c, my_x, my_z), :], got_d.at[c, part_at(c, my_x, slot), :]
             target = (me_b, other * nx + my_x)
             out.append(remote(src, dst, dz_send.at[c, other], dz_recv.at[c, slot], target))
         return out
@@ -677,7 +687,7 @@
         out = []
         for other in others(nx, my_x):
             slot = my_x if sending else other
-            src, dst = got_d.at[c, part_at(my_x, 0, nz), :], got_d.at[c, part_at(slot, 0, nz), :]
+            src, dst = got_d.at[c, part_at(c, my_x, 0, nz), :], got_d.at[c, part_at(c, slot, 0, nz), :]
             target = (me_b, my_z * nx + other)
             out.append(remote(src, dst, dx_send.at[c], dx_recv.at[c], target))
         return out
@@ -704,27 +714,29 @@
         v = got_a[c, 0].astype(F32)
         for b in range(1, nb):
             v = v + got_a[c, b].astype(F32)
-        part_s[c, 0 : sz.batch_rows, :] = v.astype(BF16)
+        for src, dst, rows in sz.moves[: 2 + c]:
+            part_s[c, dst : dst + rows, :] = v[src : src + rows].astype(BF16)
         for copy in x_copies(c):
             copy.start()
 
     def sum_third(c):
         copies = x_copies(c)
         finish((copies, copies))
-        mine = part_at(my_x, 0, nz)
+        mine = part_at(c, my_x, 0, nz)
         if nx > 1:
-            v = part_s[c, mine, :].astype(F32) + got_x[c].astype(F32)
+            v = part_s[c, mine, :].astype(F32) + got_x[c, 0 : nz * sz.part[c], :].astype(F32)
             part_s[c, mine, :] = v.astype(BF16)
         for copy in z_copies(c, True):
             copy.start()
 
     def sum_fourth(c):
         finish((z_copies(c, True), z_copies(c, False)))
-        got_z[c, my_z] = part_s[c, part_at(my_x, my_z), :]
-        v = got_z[c, 0].astype(F32)
+        span = slice(0, sz.part[c])
+        got_z[c, my_z, span, :] = part_s[c, part_at(c, my_x, my_z), :]
+        v = got_z[c, 0, span, :].astype(F32)
         for z in range(1, nz):
-            v = v + got_z[c, z].astype(F32)
-        got_d[c, part_at(my_x, my_z), :] = v.astype(BF16)
+            v = v + got_z[c, z, span, :].astype(F32)
+        got_d[c, part_at(c, my_x, my_z), :] = v.astype(BF16)
         for copy in back_z_copies(c, True):
             copy.start()
 
@@ -809,7 +821,7 @@
             nine_shifts(pltpu.roll(v, W[2], 1), W[2], store)
             return 0
 
-        lax.fori_loop(0, nb, item, 0)
+        lax.fori_loop(0, nb, item, 0, unroll=True)
         acc = None
         for b in range(nb):
             part = lax.dot_general(
@@ -973,7 +985,7 @@
                 nine_shifts(jnp.concatenate(parts, axis=1) if nz > 1 else parts[0], W[3], store)
             return 0
 
-        lax.fori_loop(0, nb, item, 0)
+        lax.fori_loop(0, nb, item, 0, unroll=True)
 
         def step(i, _):
             acc = None
@@ -1443,40 +1455,37 @@
     norm_grad(0, y1, p1)
     sum_level(0, 0, x3)
     sum_first(0, 0)
-    sum_third(1)
-    grad_third(1)
     got = ex_end(9)
     totals_ref[2] = jnp.where(jnp.concatenate([fine_place] * 2, axis=0), got_f, got)
     take_rims(3, COARSE, p1)
     norm_columns(rstd1_c * gain1_p, got, COARSE)
+    norm_grad(3, y1, p1)
+    grad_begin(0)
+    norm_grad(2, y1, p1)
+    pair_grad_begin(0)
+    sum_third(1)
     norm_grad(1, y1, p1)
     for l in sz.sum_levels[1:]:
-        if l == 2:
-            norm_grad(2, y1, p1)
         sum_level(0, l, x3)
     sum_first(0, 1)
-    if sz.pair:
-        norm_grad(2, y1, p1)
-    pair_grad_begin(0)
-    norm_grad(3, y1, p1)
-    grad_begin(0)
-    sum_fourth(1)
-
+    grad_third(1)
     conv(0, wide, 0, g3, y1, -1)
     features_out(0)
+    grad_next(0)
     pair_gradient(0)
     sum_second(0)
-    grad_next(0)
-    for l in (1, 2):
-        conv(l, wide, 0, g3, y1, -1)
-        features_out(l)
-    sum_fifth(1)
+    conv(1, wide, 0, g3, y1, -1)
+    features_out(1)
+    grad_third(0)
     sum_third(0)
+    sum_fourth(1)
+    conv(2, wide, 0, g3, y1, -1)
+    features_out(2)
     conv(3, wide, 0, g3, y1, -1)
     features_out(3)
-    grad_third(0)
     coarse_gradient(1)
     sum_fourth(0)
+    sum_fifth(1)
     coarse_gradient(0)
     sum_fifth(0)
     sum_last(1)
@@ -1653,8 +1662,8 @@
         vm((2, nb, sz.batch_rows, 128), BF16),
         vm((2, nb, sz.batch_rows, 128), BF16),
         vm((2, sz.sum_rows, 128), BF16),
-        vm((2, sz.nz * sz.part, 128), BF16),
-        vm((2, sz.nz, sz.part, 128), BF16),
+        vm((2, sz.nz * max(sz.part), 128), BF16),
+        vm((2, sz.nz, max(sz.part), 128), BF16),
         vm((2, sz.sum_rows, 128), BF16),
         pltpu.SemaphoreType.DMA((2,)),
     ]

time: 122 us -> 117 us (0.959)
  Pallas kernels: 121 us -> 116 us
    pallas_call x1, Pallas kernels: 115 us -> 110 us  [body(): pl.pallas_call(functools.partial(main_kernel, sz, nb, nk), out_shape=outs...]
where the time goes in v3:
time: 117 us; the launch traced here: 116 us
  Pallas kernels  116 us (99%)
    pallas_call x1, Pallas kernels, body(): pl.pallas_call(functools.partial(main_kernel, sz, nb, nk), out_shape=outs...  110 us
    pallas_call x1, Pallas kernels, body(): pl.pallas_call(functools.partial(last_kernel, sz, nb), out_shape=outs, in...  5.59 us

profile of v3, /device:TPU:0, one launch (start us, length us, event | category | flops | bytes accessed | tf_op | source)
XLA Modules:
  0.0 116.4 jit_solution(16540034903946977565)
XLA Ops:
  0.7 109.9 %shard_map.360 = (bf16[768,256]{1,0:T(8,128)(2,1)}, bf16[768,256]{1,0:T(8,128)(2,1)}, bf16[768,128]{1,0:T(8,128)(2,1)}, bf16[256,192]{1,0:T(8,128)(2,1)}, bf16[6...) custom-call(s32[4]{0:T(128)} %refs_0_.1, s32[4]{0:T(128)} %refs_1_.1, ...), custom_call_target="tpu_custom_call" | custom-call | tf_op jit(solution)/shard_map/pallas_call | solution.py:1705
  110.6 5.6 %shard_map.361 = (bf16[768,256]{1,0:T(8,128)(2,1)}, bf16[768,256]{1,0:T(8,128)(2,1)}, bf16[768,128]{1,0:T(8,128)(2,1)}, bf16[256,192]{1,0:T(8,128)(2,1)}, bf16[6...) custom-call(bf16[768,256]{1,0:T(8,128)(2,1)} %get-tuple-element.40.r, ...), custom_call_target="tpu_custom_call" | custom-call | tf_op jit(solution)/shard_map/pallas_call | solution.py:1735

commit v4 on v3

--- a/solution.py
+++ b/solution.py
@@ -128,8 +128,7 @@
     norm_gains, norm_shifts, unite_gains, unite_shifts = take(4)
     tables = take(3)
     tables_t = take(3)
-    (united_ref,) = take(1)
-    gfeat = take(4)
+    map_outs = take(5)
     (sums_ref,) = take(1)
     (coarse_ref,) = take(1)
     (totals_ref,) = take(1)
@@ -155,6 +154,12 @@
     (rec_a, rec_b, rim_s, rim_r, mid_s, mid_r) = take(6)
     (sa_send, sa_recv, sb_send, sb_recv, rim_send, rim_recv) = take(6)
     raw_sem, wide_sem = take(2)
+    united_ref, *gfeat = take(5)
+    (map_sem,) = take(1)
+
+    def map_copy(i):
+        return pltpu.make_async_copy(([united_ref] + gfeat)[i], map_outs[i], map_sem.at[i])
+
     prow, urow = take(2)
     part_a, got_a, part_s, got_x, got_z, got_d, out_sem = take(7)
     (ra_send, ra_recv, rx_send, rx_recv, rz_send, rz_recv) = take(6)
@@ -1173,6 +1178,7 @@
         if W[l] < 128:
             v = jnp.where(masks[l][1:2, :] > 0, y1[l][...] + xf[l][...], 0.0)
             gfeat[l][...] = pltpu.roll(v, NP[l] - W[l], 1).T[0 : N[l]].astype(BF16)
+            map_copy(1 + l).start()
             return
 
         def body(r0, rc, lanes):
@@ -1186,6 +1192,7 @@
         each(l, body)
         for h in range(halves(l)):
             gfeat[l][:, 128 * h : 128 * h + 128] = stage[h].astype(BF16)
+        map_copy(1 + l).start()
 
     sizes, u_sizes = (n_a, n_b), (un_a, un_b)
     fine_place = place < C[0]
@@ -1327,6 +1334,7 @@
     lax.fori_loop(0, UC_ // 16, total_step, 0)
     for h in range(halves(0)):
         united_ref[:, 128 * h : 128 * h + 128] = stage[h].astype(BF16)
+    map_copy(0).start()
 
     for j in range(3):
         l = j + 1
@@ -1492,6 +1500,8 @@
     sum_last(0)
     for c in range(2):
         pltpu.make_async_copy(got_d.at[c], sums_ref.at[c], out_sem.at[c]).wait()
+    for i in range(5):
+        map_copy(i).wait()
 
 
 def last_kernel(sz, nb, *refs):
@@ -1657,6 +1667,8 @@
         pltpu.SemaphoreType.DMA((9, 2)),
         pltpu.SemaphoreType.DMA((4, 2)),
         pltpu.SemaphoreType.DMA((2, 9)),
+        *[vm(m, BF16) for m in map_shapes],
+        pltpu.SemaphoreType.DMA((5,)),
         vm((8, sz.blocks * 128), F32),
         vm((8, sz.ublocks * 128), F32),
         vm((2, nb, sz.batch_rows, 128), BF16),
@@ -1709,8 +1721,7 @@
         + [in_vmem] * 5
         + [pl.BlockSpec(memory_space=pl.ANY)] * 4
         + [in_vmem] * (len(operands) - 12),
-        out_specs=[in_vmem] * 5
-        + [pl.BlockSpec(memory_space=pl.ANY)] * 2
+        out_specs=[pl.BlockSpec(memory_space=pl.ANY)] * 7
         + [in_vmem],
         scratch_shapes=scratch,
         compiler_params=pltpu.CompilerParams(

time: 117 us -> 116 us (level)
  no operation moved by 1% of the time
where the time goes in v4:
time: 116 us
  Pallas kernels  115 us (99%)
    pallas_call x1, Pallas kernels, body(): pl.pallas_call(functools.partial(main_kernel, sz, nb, nk), out_shape=outs...  110 us
    pallas_call x1, Pallas kernels, body(): pl.pallas_call(functools.partial(last_kernel, sz, nb), out_shape=outs, in...  5.59 us

profile of v4, /device:TPU:0, one launch (start us, length us, event | category | flops | bytes accessed | tf_op | source)
XLA Modules:
  0.0 116.0 jit_solution(388722321776097295)
XLA Ops:
  0.7 109.6 %shard_map.360 = (bf16[768,256]{1,0:T(8,128)(2,1)}, bf16[768,256]{1,0:T(8,128)(2,1)}, bf16[768,128]{1,0:T(8,128)(2,1)}, bf16[256,192]{1,0:T(8,128)(2,1)}, bf16[6...) custom-call(s32[4]{0:T(128)} %refs_0_.1, s32[4]{0:T(128)} %refs_1_.1, ...), custom_call_target="tpu_custom_call" | custom-call | tf_op jit(solution)/shard_map/pallas_call | solution.py:1717
  110.2 5.6 %shard_map.361 = (bf16[768,256]{1,0:T(8,128)(2,1)}, bf16[768,256]{1,0:T(8,128)(2,1)}, bf16[768,128]{1,0:T(8,128)(2,1)}, bf16[256,192]{1,0:T(8,128)(2,1)}, bf16[6...) custom-call(bf16[768,256]{1,0:T(8,128)(2,1)} %get-tuple-element.40.r, ...), custom_call_target="tpu_custom_call" | custom-call | tf_op jit(solution)/shard_map/pallas_call | solution.py:1746
